TPU v7x, 32 devices: a whole 2x2x4 slice. The times are simulated.
32 devices in a mesh: seq: 16 (over z, y, x), head: 2 (over core).
Axes of the slice: x: 2, y: 2, z: 4, core: 2. Of those that a mesh axis runs over, the one named last changes fastest.
Arguments:
- tokens: bfloat16 [16384, 768], P('seq'), may hold values from -6 to 6
- out_grad: bfloat16 [16384, 768], P('seq'), may hold values from -6 to 6
- doc_lengths: int32 [15], replicated, may hold values from 1 to 2048, as said below
- cluster_perm: int32 [16384], P('seq'), may hold values from 0 to 2047, as said below
- query_weight: bfloat16 [768, 768], P(None, 'head'), may hold values from -0.21875 to 0.21875
- query_bias: float32 [768], P('head'), may hold values from -3 to 3
- key_weight: bfloat16 [768, 768], P(None, 'head'), may hold values from -0.21875 to 0.21875
- value_weight: bfloat16 [768, 768], P(None, 'head'), may hold values from -0.21875 to 0.21875
- value_bias: float32 [768], P('head'), may hold values from -3 to 3
- output_weight: bfloat16 [768, 768], P('head'), may hold values from -0.875 to 0.875
- output_bias: float32 [768], replicated, may hold values from -3 to 3
- first_gain: float32 [768], replicated, may hold values from 0.1 to 1.9
- first_shift: float32 [768], replicated, may hold values from -3 to 3
- up_weight: bfloat16 [768, 3072], P(None, 'head'), may hold values from -0.21875 to 0.21875
- up_bias: float32 [3072], P('head'), may hold values from -3 to 3
- down_weight: bfloat16 [3072, 768], P('head'), may hold values from -0.109375 to 0.109375
- down_bias: float32 [768], replicated, may hold values from -3 to 3
- second_gain: float32 [768], replicated, may hold values from 0.1 to 1.9
- second_shift: float32 [768], replicated, may hold values from -3 to 3
Outputs:
- layer_out: float32 [16384, 768], P('seq')
- input_grad: float32 [16384, 768], P('seq')
- query_weight_grad: float32 [768, 768], P('seq', 'head')
- query_bias_grad: float32 [768], P('head')
- key_weight_grad: float32 [768, 768], P('seq', 'head')
- value_weight_grad: float32 [768, 768], P('seq', 'head')
- value_bias_grad: float32 [768], P('head')
- output_weight_grad: float32 [768, 768], P('head', 'seq')
- output_bias_grad: float32 [768], P('seq')
- first_gain_grad: float32 [768], P('seq')
- first_shift_grad: float32 [768], P('seq')
- up_weight_grad: float32 [768, 3072], P('seq', 'head')
- up_bias_grad: float32 [3072], P('head')
- down_weight_grad: float32 [3072, 768], P('head', 'seq')
- down_bias_grad: float32 [768], P('seq')
- second_gain_grad: float32 [768], P('seq')
- second_shift_grad: float32 [768], P('seq')
Inputs may be any that keep to these rules, and one draw needn't show every extreme that they name: `doc_lengths`: document i occupies its length rounded up to a multiple of 128 positions; the documents lie end to end from position 0 and fill all 16384 positions; positions past a length in its last cluster are padding. `cluster_perm`: within each document of padded length P, the values at its positions are a permutation of 0 to P - 1.
All inputs are finite; a program needn't handle non-finite values.
Results may differ from a plain program's by a relative error of at most 0.014.
The roundings to bfloat16 on the way count: a program that leaves them out, or rounds other values in their place, can miss the bound.
Values may be sent and summed in bfloat16 or wider, within the bound.
A program may use at most 128 MiB of HBM per device.

v0:
```python
import jax
import jax.numpy as jnp
from jax import lax
from jax.sharding import PartitionSpec as P

HEAD_DIM = 64
CLUSTER = 128
SPAN = 2


norm_eps = 1e-12
masked_score = -1e30
root_half = 0.7071067811865476
inv_root_tau = 0.3989422804014327


def passed_along(value, axis, steps):
    count = lax.axis_size(axis)
    leading, last = (max(0, -steps), min(count, count - steps))
    return lax.ppermute(value, axis, [(source, source + steps) for source in range(leading, last)])


def doc_lookup(doc_lengths, positions):
    padded = (doc_lengths + CLUSTER - 1) // CLUSTER * CLUSTER
    starts = jnp.cumsum(padded) - padded
    doc_of = jnp.sum((starts[None, :] <= positions[:, None]).astype(jnp.int32), axis=1) - 1
    picked = jnp.arange(starts.shape[0], dtype=jnp.int32)[None, :] == doc_of[:, None]
    slot_start = jnp.sum(jnp.where(picked, starts[None, :], 0), axis=1)
    slot_length = jnp.sum(jnp.where(picked, doc_lengths[None, :], 0), axis=1)
    return (slot_start, slot_length)


def norm_forward(values, gain, shift):
    row_mean = jnp.mean(values, axis=-1, keepdims=True)
    centered = values - row_mean
    inv_std = lax.rsqrt(jnp.mean(centered * centered, axis=-1, keepdims=True) + norm_eps)
    normed = centered * inv_std
    return (normed * gain + shift, normed, inv_std)


def norm_backward(grad_out, normed, inv_std, gain):
    scaled = grad_out * gain
    return inv_std * (
        scaled
        - jnp.mean(scaled, axis=-1, keepdims=True)
        - normed * jnp.mean(scaled * normed, axis=-1, keepdims=True)
    )


def inner_rows(left, right):
    return lax.dot_general(
        left, right, (((0,), (0,)), ((), ())), preferred_element_type=jnp.float32
    )


def outer_cols(left, right):
    return lax.dot_general(
        left, right, (((1,), (1,)), ((), ())), preferred_element_type=jnp.float32
    )


def split_heads(rows):
    clusters = rows.shape[0] // CLUSTER
    return rows.reshape(clusters, CLUSTER, rows.shape[1] // HEAD_DIM, HEAD_DIM)


def masked_scores(query_slot, key_slot, key_valid):
    scores = jnp.einsum(
        "gqhd,gkhd->ghqk",
        split_heads(query_slot),
        split_heads(key_slot),
        preferred_element_type=jnp.float32,
    ) * HEAD_DIM ** (-0.5)
    valid_keys = key_valid.reshape(scores.shape[0], 1, 1, CLUSTER)
    return jnp.where(valid_keys, scores, masked_score)


def body(
    tokens,
    out_grad,
    doc_lengths,
    cluster_perm,
    query_weight,
    query_bias,
    key_weight,
    value_weight,
    value_bias,
    output_weight,
    output_bias,
    first_gain,
    first_shift,
    up_weight,
    up_bias,
    down_weight,
    down_bias,
    second_gain,
    second_shift,
):
    tok_rows = tokens.shape[0]
    block_index = lax.axis_index("seq")
    positions = block_index * tok_rows + jnp.arange(tok_rows, dtype=jnp.int32)
    slot_start, slot_length = doc_lookup(doc_lengths, positions)
    window_row = slot_start + cluster_perm - (block_index - SPAN) * tok_rows
    key_valid = cluster_perm < slot_length
    span_rows = (2 * SPAN + 1) * tok_rows
    joined_weight = jnp.stack((query_weight, key_weight, value_weight))
    joined_bias = jnp.stack((query_bias, jnp.zeros_like(query_bias), value_bias))
    projected = jnp.einsum("td,sde->ste", tokens, joined_weight, preferred_element_type=jnp.float32)
    local_rows = (projected + joined_bias[:, None, :]).astype(jnp.bfloat16)
    pulled = {0: local_rows}
    for offset in range(1, SPAN + 1):
        for direction in (1, -1):
            pulled[direction * offset] = passed_along(local_rows, "seq", -direction * offset)
    window = jnp.concatenate([pulled[offset] for offset in range(-SPAN, SPAN + 1)], axis=1)
    slot_rows = jnp.take(window, window_row, axis=1)
    scores = masked_scores(slot_rows[0], slot_rows[1], key_valid)
    row_max = jnp.max(scores, axis=-1, keepdims=True)
    raw_weight = jnp.exp(scores - row_max)
    row_total = jnp.sum(raw_weight, axis=-1, keepdims=True)
    log_total = row_max + jnp.log(row_total)
    prob_low = (raw_weight / row_total).astype(jnp.bfloat16)
    context = jnp.einsum(
        "ghqk,gkhd->gqhd", prob_low, split_heads(slot_rows[2]), preferred_element_type=jnp.float32
    )
    context_slot = context.astype(jnp.bfloat16).reshape(tok_rows, -1)
    home_buffer = (
        jnp.zeros((span_rows, context_slot.shape[1]), jnp.bfloat16).at[window_row].set(context_slot)
    )
    context_sum = home_buffer[SPAN * tok_rows : (SPAN + 1) * tok_rows].astype(jnp.float32)
    for offset in range(-SPAN, SPAN + 1):
        if offset != 0:
            piece = home_buffer[(offset + SPAN) * tok_rows : (offset + SPAN + 1) * tok_rows]
            context_sum = context_sum + passed_along(piece, "seq", offset).astype(jnp.float32)
    context_home = context_sum.astype(jnp.bfloat16)
    attn_out = lax.psum(
        jnp.dot(context_home, output_weight, preferred_element_type=jnp.float32), "head"
    )
    hidden = tokens.astype(jnp.float32) + attn_out + output_bias
    first_norm, first_hat, first_inv = norm_forward(hidden, first_gain, first_shift)
    first_low = first_norm.astype(jnp.bfloat16)
    pre_act = jnp.dot(first_low, up_weight, preferred_element_type=jnp.float32) + up_bias
    normal_cdf = 0.5 * (1.0 + lax.erf(pre_act * root_half))
    activation = (pre_act * normal_cdf).astype(jnp.bfloat16)
    ffn_out = lax.psum(jnp.dot(activation, down_weight, preferred_element_type=jnp.float32), "head")
    summed = first_norm + ffn_out + down_bias
    layer_out, second_hat, second_inv = norm_forward(summed, second_gain, second_shift)
    grad_out = out_grad.astype(jnp.float32)
    second_gain_grad = jnp.sum(grad_out * second_hat, axis=0)
    second_shift_grad = jnp.sum(grad_out, axis=0)
    summed_grad = norm_backward(grad_out, second_hat, second_inv, second_gain)
    down_bias_grad = jnp.sum(summed_grad, axis=0)
    ffn_low = summed_grad.astype(jnp.bfloat16)
    down_weight_grad = inner_rows(activation, ffn_low)
    act_grad = outer_cols(ffn_low, down_weight)
    slope = normal_cdf + pre_act * jnp.exp(-0.5 * pre_act * pre_act) * inv_root_tau
    pre_grad = (act_grad * slope).astype(jnp.bfloat16)
    up_bias_part = jnp.sum(pre_grad.astype(jnp.float32), axis=0)
    up_weight_grad = inner_rows(first_low, pre_grad)
    first_grad = lax.psum(outer_cols(pre_grad, up_weight), "head") + summed_grad
    first_gain_grad = jnp.sum(first_grad * first_hat, axis=0)
    first_shift_grad = jnp.sum(first_grad, axis=0)
    hidden_grad = norm_backward(first_grad, first_hat, first_inv, first_gain)
    output_bias_grad = jnp.sum(hidden_grad, axis=0)
    attn_low = hidden_grad.astype(jnp.bfloat16)
    output_weight_grad = inner_rows(context_home, attn_low)
    context_grad = outer_cols(attn_low, output_weight).astype(jnp.bfloat16)
    pulled_grad = {0: context_grad}
    for offset in range(1, SPAN + 1):
        for direction in (1, -1):
            pulled_grad[direction * offset] = passed_along(context_grad, "seq", -direction * offset)
    grad_span = jnp.concatenate([pulled_grad[offset] for offset in range(-SPAN, SPAN + 1)], axis=0)
    slot_grad = jnp.take(grad_span, window_row, axis=0)
    attn_prob = jnp.exp(masked_scores(slot_rows[0], slot_rows[1], key_valid) - log_total)
    grad_heads = split_heads(slot_grad)
    prob_grad = jnp.einsum(
        "gqhd,gkhd->ghqk", grad_heads, split_heads(slot_rows[2]), preferred_element_type=jnp.float32
    )
    score_grad = (
        attn_prob * (prob_grad - jnp.sum(attn_prob * prob_grad, axis=-1, keepdims=True))
    ).astype(jnp.bfloat16)
    score_scale = HEAD_DIM ** (-0.5)
    query_grad = (
        jnp.einsum(
            "ghqk,gkhd->gqhd",
            score_grad,
            split_heads(slot_rows[1]),
            preferred_element_type=jnp.float32,
        )
        * score_scale
    )
    key_grad = (
        jnp.einsum(
            "ghqk,gqhd->gkhd",
            score_grad,
            split_heads(slot_rows[0]),
            preferred_element_type=jnp.float32,
        )
        * score_scale
    )
    value_grad = jnp.einsum(
        "ghqk,gqhd->gkhd", prob_low, grad_heads, preferred_element_type=jnp.float32
    )
    slot_grads = (
        jnp.stack((query_grad, key_grad, value_grad)).astype(jnp.bfloat16).reshape(3, tok_rows, -1)
    )
    grad_buffer = (
        jnp.zeros((3, span_rows, slot_grads.shape[2]), jnp.bfloat16)
        .at[:, window_row]
        .set(slot_grads)
    )
    home_grads = grad_buffer[:, SPAN * tok_rows : (SPAN + 1) * tok_rows].astype(jnp.float32)
    for offset in range(-SPAN, SPAN + 1):
        if offset != 0:
            piece = grad_buffer[:, (offset + SPAN) * tok_rows : (offset + SPAN + 1) * tok_rows]
            home_grads = home_grads + passed_along(piece, "seq", offset).astype(jnp.float32)
    home_low = home_grads.astype(jnp.bfloat16)
    projected_grad = jnp.einsum("td,ste->sde", tokens, home_low, preferred_element_type=jnp.float32)
    input_part = jnp.einsum(
        "ste,sde->td", home_low, joined_weight, preferred_element_type=jnp.float32
    )
    input_grad = lax.psum(input_part.astype(jnp.bfloat16), "head").astype(jnp.float32) + hidden_grad
    bias_parts = jnp.sum(home_grads, axis=1)
    query_bias_grad, value_bias_grad, up_bias_grad = lax.psum(
        (bias_parts[0], bias_parts[2], up_bias_part), "seq"
    )
    summed_grads = (
        lax.psum_scatter(projected_grad, "seq", scatter_dimension=1, tiled=True),
        lax.psum_scatter(output_weight_grad, "seq", scatter_dimension=1, tiled=True),
        lax.psum_scatter(up_weight_grad, "seq", scatter_dimension=0, tiled=True),
        lax.psum_scatter(down_weight_grad, "seq", scatter_dimension=1, tiled=True),
        lax.psum_scatter(output_bias_grad, "seq", scatter_dimension=0, tiled=True),
        lax.psum_scatter(first_gain_grad, "seq", scatter_dimension=0, tiled=True),
        lax.psum_scatter(first_shift_grad, "seq", scatter_dimension=0, tiled=True),
        lax.psum_scatter(down_bias_grad, "seq", scatter_dimension=0, tiled=True),
        lax.psum_scatter(second_gain_grad, "seq", scatter_dimension=0, tiled=True),
        lax.psum_scatter(second_shift_grad, "seq", scatter_dimension=0, tiled=True),
    )
    return (
        layer_out,
        input_grad,
        summed_grads[0][0],
        query_bias_grad,
        summed_grads[0][1],
        summed_grads[0][2],
        value_bias_grad,
        summed_grads[1],
        summed_grads[4],
        summed_grads[5],
        summed_grads[6],
        summed_grads[2],
        up_bias_grad,
        summed_grads[3],
        summed_grads[7],
        summed_grads[8],
        summed_grads[9],
    )


def solution(mesh):
    placed = (
        P("seq", None),
        P("seq", None),
        P(),
        P("seq"),
        P(None, "head"),
        P("head"),
        P(None, "head"),
        P(None, "head"),
        P("head"),
        P("head", None),
        P(),
        P(),
        P(),
        P(None, "head"),
        P("head"),
        P("head", None),
        P(),
        P(),
        P(),
    )
    return jax.shard_map(
        body,
        mesh=mesh,
        in_specs=placed,
        out_specs=(
            P("seq", None),
            P("seq", None),
            P("seq", "head"),
            P("head"),
            P("seq", "head"),
            P("seq", "head"),
            P("head"),
            P("head", "seq"),
            P("seq"),
            P("seq"),
            P("seq"),
            P("seq", "head"),
            P("head"),
            P("head", "seq"),
            P("seq"),
            P("seq"),
            P("seq"),
        ),
        check_vma=False,
    )
```

profile of v0, /device:TPU:0, one launch (start us, length us, event | category | flops | bytes accessed | tf_op | source)
XLA Modules:
  0.0 1463.9 jit_solution(11384901516360029501)
XLA Ops:
  14.1 5.1 fusion.15
  19.2 6.3 collective-permute-start
  25.5 4.8 collective-permute-start.1
  33.6 142.4 %collective-permute-done = bf16[3,1024,384]{1,2,0:T(8,128)(2,1)} collective-permute-done((bf16[3,1024,384]{1,2,0:T(8,128)(2,1)}, bf16[3,1024,384]{1,2,0:T(8,128)(2,1)}, u32[]{:S(2)}, u32[]{:S(2)}) %collective-permute-start) | collective-permute-done | bytes 2359328 | tf_op jit(solution)/shard_map/ppermute | solution.py:20
  192.9 23.8 %copy.189 = bf16[3,5120,384]{2,0,1:T(4,128)(2,1)} copy(bf16[3,5120,384]{1,2,0:T(8,128)(2,1)} %constant_dynamic-update-slice_fusion) | data formatting | bytes 23592960 | tf_op jit(solution)/shard_map/concatenate | solution.py:114
  216.7 15.4 %gather_fusion = bf16[1024,3,384]{2,1,0:T(4,128)(2,1)} fusion(bf16[3,5120,384]{2,0,1:T(4,128)(2,1)} %copy.189, s32[1024]{0:T(1024)S(1)} %broadcast_clamp_fusion), kind=kCustom, calls=%fused_computation | custom fusion | bytes 4722688 | tf_op jit(solution)/shard_map/jit(_take)/gather | solution.py:115
  232.1 5.5 select_bitcast_fusion
  237.6 4.9 fusion.56
  242.5 4.7 copy.190
  248.5 4.9 copy.192
  255.6 4.7 copy.191
  268.7 8.2 scatter_custom_fusion
  280.5 5.1 collective-permute-start.7
  290.4 9.9 collective-permute-done.4
  300.3 33.9 %collective-permute-done.7 = bf16[1024,384]{1,0:T(8,128)(2,1)S(1)} collective-permute-done((bf16[1024,384]{1,0:T(8,128)(2,1)S(1)}, bf16[1024,384]{1,0:T(8,128)(2,1)S(1)}, u32[]{:S(2)}, u32[]{:S(2)}) %collective-permute-start.7) | collective-permute-done | bytes 786464 | tf_op jit(solution)/shard_map/ppermute | solution.py:20
  339.6 23.5 %all-reduce.14.cloned.1.call-done = f32[1024,768]{1,0:T(8,128)} async-done(((f32[1024,768]{1,0:T(8,128)}), f32[1024,768]{1,0:T(8,128)}) %all-reduce.14.cloned.1.call-update) | async-done | bytes 3145744 | tf_op jit(solution)/shard_map/psum | solution.py:135
  366.7 5.1 multiply_convert_fusion
  373.5 4.3 fusion.59
  378.2 24.1 %all-reduce.16.cloned.1.call-done = f32[1024,768]{1,0:T(8,128)} async-done(((f32[1024,768]{1,0:T(8,128)}), f32[1024,768]{1,0:T(8,128)}) %all-reduce.16.cloned.1.call-update) | async-done | bytes 3145744 | tf_op jit(solution)/shard_map/psum | solution.py:144
  402.3 3.9 fusion.52
  412.9 4.7 convert_reduce_fusion
  419.3 4.3 fusion.60
  423.7 24.5 %all-reduce.18.cloned.1.call-done = f32[1024,768]{1,0:T(8,128)} async-done(((f32[1024,768]{1,0:T(8,128)}), f32[1024,768]{1,0:T(8,128)}) %all-reduce.18.cloned.1.call-update) | async-done | bytes 3145744 | tf_op jit(solution)/shard_map/psum | solution.py:159
  448.1 4.7 multiply_reduce_fusion
  456.5 3.7 collective-permute-start.8
  466.2 28.0 %collective-permute-done.8 = bf16[1024,384]{1,0:T(8,128)(2,1)S(1)} collective-permute-done((bf16[1024,384]{1,0:T(8,128)(2,1)S(1)}, bf16[1024,384]{1,0:T(8,128)(2,1)S(1)}, u32[]{:S(2)}, u32[]{:S(2)}) %collective-permute-start.8) | collective-permute-done | bytes 786464 | tf_op jit(solution)/shard_map/ppermute | solution.py:20
  501.2 6.6 gather_fusion.1
  524.5 3.9 copy.211
  528.4 5.8 broadcast_in_dim.102
  534.2 114.5 %scatter_fusion = bf16[3,5120,384]{2,0,1:T(4,128)(2,1)} fusion(bf16[3,5120,384]{2,0,1:T(4,128)(2,1)} %broadcast_in_dim.102, s32[1024]{0:T(1024)S(1)} %get-tuple-element.101, bf16[1024,3,384]{2,1,0:T(4,128)(2,1)} %copy.211), kind=kCustom, calls=%fused_computation.3 | custom fusion | bytes 7081984 | tf_op jit(solution)/shard_map/scatter | solution.py:209
  648.7 8.6 fusion.54
  661.5 18.9 %collective-permute-start.14 = (bf16[3,1024,384]{2,1,0:T(8,128)(2,1)S(1)}, bf16[3,1024,384]{2,1,0:T(8,128)(2,1)S(1)}, u32[]{:S(2)}, u32[]{:S(2)}) collective-permute-start(bf16[3,1024,384]{2,1,0:T(8,128)(2,1)S(1)} %copy.215), channel_id=1, source_target_pairs={{0,2},{2,4},{4,6},{6,8},{8,10},{10,12},{12,14},{14,16},{16,18},{18... | collective-permute-start | bytes 7077896 | tf_op jit(solution)/shard_map/ppermute | solution.py:20
  680.4 5.1 collective-permute-start.15
  685.6 40.1 %collective-permute-done.12 = bf16[3,1024,384]{2,1,0:T(8,128)(2,1)S(1)} collective-permute-done((bf16[3,1024,384]{2,1,0:T(8,128)(2,1)S(1)}, bf16[3,1024,384]{2,1,0:T(8,128)(2,1)S(1)}, u32[]{:S(2)}, u32[]{:S(2)}) %collective-permute-start.12) | collective-permute-done | bytes 2359328 | tf_op jit(solution)/shard_map/ppermute | solution.py:20
  725.7 4.8 collective-permute-done.13
  730.5 50.5 %collective-permute-done.14 = bf16[3,1024,384]{2,1,0:T(8,128)(2,1)S(1)} collective-permute-done((bf16[3,1024,384]{2,1,0:T(8,128)(2,1)S(1)}, bf16[3,1024,384]{2,1,0:T(8,128)(2,1)S(1)}, u32[]{:S(2)}, u32[]{:S(2)}) %collective-permute-start.14) | collective-permute-done | bytes 2359328 | tf_op jit(solution)/shard_map/ppermute | solution.py:20
  781.0 46.0 %collective-permute-done.15 = bf16[3,1024,384]{2,1,0:T(8,128)(2,1)S(1)} collective-permute-done((bf16[3,1024,384]{2,1,0:T(8,128)(2,1)S(1)}, bf16[3,1024,384]{2,1,0:T(8,128)(2,1)S(1)}, u32[]{:S(2)}, u32[]{:S(2)}) %collective-permute-start.15) | collective-permute-done | bytes 2359328 | tf_op jit(solution)/shard_map/ppermute | solution.py:20
  831.9 5.2 convolution_bitcast_fusion
  837.2 6.4 copy.219
  843.7 4.1 fusion.26
  847.8 7.7 fusion.29
  855.9 7.9 fusion.44
  865.8 78.9 %all-reduce.7 = (f32[384]{0:T(512)}, f32[384]{0:T(512)}, f32[768]{0:T(1024)S(1)}, f32[768]{0:T(1024)S(1)}, f32[768]{0:T(1024)S(1)}, /*index=5*/f32[1536]{0:T(102...) all-reduce(f32[384]{0:T(512)S(1)} %get-tuple-element.77, ...), channel_id=1, replica_groups=mesh['seq'=16,'head'=2] {'seq'}, use_global_device_ids=true, to_apply=%region_23.24 | all-reduce | flops 6912 | bytes 55296 | tf_op jit(solution)/shard_map/psum | solution.py:223
  948.2 4.5 convert_add_fusion.1
  952.7 91.1 %all-reduce.22.cloned.1.call-done = f32[3,768,384]{2,0,1:T(4,128)} async-done(((f32[3,768,384]{2,0,1:T(4,128)}), f32[3,768,384]{2,0,1:T(4,128)}) %all-reduce.22.cloned.1.call-update) | async-done | bytes 3538960
  1047.1 125.2 %reduce-scatter.4.cloned.1.call-done = f32[384,48]{0,1:T(8,128)} async-done(((f32[384,768]{0,1:T(8,128)}), f32[384,48]{0,1:T(8,128)}) %reduce-scatter.4.cloned.1.call-update) | async-done | bytes 73744 | tf_op jit(solution)/shard_map/reduce_scatter | solution.py:228
  1172.3 143.1 %reduce-scatter.8.cloned.1.call-done = f32[1536,48]{0,1:T(8,128)} async-done(((f32[1536,768]{0,1:T(8,128)}), f32[1536,48]{0,1:T(8,128)}) %reduce-scatter.8.cloned.1.call-update) | async-done | bytes 294928 | tf_op jit(solution)/shard_map/reduce_scatter | solution.py:230
  1315.4 141.4 %reduce-scatter.6.cloned.1.call-done = f32[48,1536]{1,0:T(8,128)} async-done(((f32[768,1536]{1,0:T(8,128)}), f32[48,1536]{1,0:T(8,128)}) %reduce-scatter.6.cloned.1.call-update) | async-done | bytes 294928 | tf_op jit(solution)/shard_map/reduce_scatter | solution.py:229
  (203 shorter events, 117.4 us)
Async XLA Ops:
  7.2 359.3 %copy-start = (bf16[768,1536]{1,0:T(8,128)(2,1)S(1)}, bf16[768,1536]{1,0:T(8,128)(2,1)}, u32[]{:S(2)}) copy-start(bf16[768,1536]{1,0:T(8,128)(2,1)} %param.32) | copy-start | bytes 7077892
  7.2 355.8 %all-reduce.14.cloned.1.call-start = ((), (), s32[]{:S(2)}) async-start(), calls=%async_computation.3 | async-start | bytes 6291456 | tf_op jit(solution)/shard_map/psum | solution.py:135
  10.1 9.1 copy-start.19
  11.6 7.6 copy-start.21
  14.1 19.0 %copy-start.31 = (s32[15]{0:T(128)S(1)}, s32[15]{0:T(128)}, u32[]{:S(2)}) copy-start(s32[15]{0:T(128)} %param.21) | copy-start | bytes 184
  14.1 19.4 %copy-start.30 = (s32[1024]{0:T(1024)S(1)}, s32[1024]{0:T(1024)}, u32[]{:S(2)}) copy-start(s32[1024]{0:T(1024)} %param.22) | copy-start | bytes 12292
  19.2 156.8 %collective-permute-start = (bf16[3,1024,384]{1,2,0:T(8,128)(2,1)}, bf16[3,1024,384]{1,2,0:T(8,128)(2,1)}, u32[]{:S(2)}, u32[]{:S(2)}) collective-permute-start(bf16[3,1024,384]{1,2,0:T(8,128)(2,1)} %fusion.15), channel_id=1, source_target_pairs={{0,4},{2,6},{4,8},{6,10},{8,12},{10,14},{12,16},{14,18},{16,20},{1... | collective-permute-start | bytes 7077896 | tf_op jit(solution)/shard_map/ppermute | solution.py:20
  25.5 153.8 %collective-permute-start.1 = (bf16[3,1024,384]{1,2,0:T(8,128)(2,1)}, bf16[3,1024,384]{1,2,0:T(8,128)(2,1)}, u32[]{:S(2)}, u32[]{:S(2)}) collective-permute-start(bf16[3,1024,384]{1,2,0:T(8,128)(2,1)} %fusion.15), channel_id=1, source_target_pairs={{0,2},{2,4},{4,6},{6,8},{8,10},{10,12},{12,14},{14,16},{16,18},{18... | collective-permute-start | bytes 7077896 | tf_op jit(solution)/shard_map/ppermute | solution.py:20
  30.4 155.7 %collective-permute-start.2 = (bf16[3,1024,384]{1,2,0:T(8,128)(2,1)}, bf16[3,1024,384]{1,2,0:T(8,128)(2,1)}, u32[]{:S(2)}, u32[]{:S(2)}) collective-permute-start(bf16[3,1024,384]{1,2,0:T(8,128)(2,1)} %fusion.15), channel_id=1, source_target_pairs={{2,0},{4,2},{6,4},{8,6},{10,8},{12,10},{14,12},{16,14},{18,16},{20... | collective-permute-start | bytes 7077896 | tf_op jit(solution)/shard_map/ppermute | solution.py:20
  31.6 157.8 %collective-permute-start.3 = (bf16[3,1024,384]{1,2,0:T(8,128)(2,1)}, bf16[3,1024,384]{1,2,0:T(8,128)(2,1)}, u32[]{:S(2)}, u32[]{:S(2)}) collective-permute-start(bf16[3,1024,384]{1,2,0:T(8,128)(2,1)} %fusion.15), channel_id=1, source_target_pairs={{4,0},{6,2},{8,4},{10,6},{12,8},{14,10},{16,12},{18,14},{20,16},{2... | collective-permute-start | bytes 7077896 | tf_op jit(solution)/shard_map/ppermute | solution.py:20
  248.5 17.8 %copy-start.9 = (bf16[48,8,8,128]{3,2,1,0:T(8,128)(2,1)}, bf16[48,8,8,128]{3,2,1,0:T(8,128)(2,1)S(1)}, u32[]{:S(2)}) copy-start(bf16[48,8,8,128]{3,2,1,0:T(8,128)(2,1)S(1)} %copy.230) | copy-start | bytes 2359300
  279.1 57.7 %copy-start.17 = (bf16[384,768]{1,0:T(8,128)(2,1)S(1)}, bf16[384,768]{1,0:T(8,128)(2,1)}, u32[]{:S(2)}) copy-start(bf16[384,768]{1,0:T(8,128)(2,1)} %param.28) | copy-start | bytes 1769476
  279.1 21.2 %collective-permute-start.4 = (bf16[1024,384]{1,0:T(8,128)(2,1)S(1)}, bf16[1024,384]{1,0:T(8,128)(2,1)S(1)}, u32[]{:S(2)}, u32[]{:S(2)}) collective-permute-start(bf16[1024,384]{1,0:T(8,128)(2,1)S(1)} %get-tuple-element.110), channel_id=1, source_target_pairs={{4,0},{6,2},{8,4},{10,6},{12,8},{14,10},{16,12},{18,14},{20,16},{2... | collective-permute-start | bytes 2359304 | tf_op jit(solution)/shard_map/ppermute | solution.py:20
  280.5 53.6 %collective-permute-start.7 = (bf16[1024,384]{1,0:T(8,128)(2,1)S(1)}, bf16[1024,384]{1,0:T(8,128)(2,1)S(1)}, u32[]{:S(2)}, u32[]{:S(2)}) collective-permute-start(bf16[1024,384]{1,0:T(8,128)(2,1)S(1)} %get-tuple-element.111), channel_id=1, source_target_pairs={{0,4},{2,6},{4,8},{6,10},{8,12},{10,14},{12,16},{14,18},{16,20},{1... | collective-permute-start | bytes 2359304 | tf_op jit(solution)/shard_map/ppermute | solution.py:20
  285.6 48.5 %collective-permute-start.6 = (bf16[1024,384]{1,0:T(8,128)(2,1)S(1)}, bf16[1024,384]{1,0:T(8,128)(2,1)S(1)}, u32[]{:S(2)}, u32[]{:S(2)}) collective-permute-start(bf16[1024,384]{1,0:T(8,128)(2,1)S(1)} %get-tuple-element.112), channel_id=1, source_target_pairs={{0,2},{2,4},{4,6},{6,8},{8,10},{10,12},{12,14},{14,16},{16,18},{18... | collective-permute-start | bytes 2359304 | tf_op jit(solution)/shard_map/ppermute | solution.py:20
  289.1 46.1 %collective-permute-start.5 = (bf16[1024,384]{1,0:T(8,128)(2,1)S(1)}, bf16[1024,384]{1,0:T(8,128)(2,1)S(1)}, u32[]{:S(2)}, u32[]{:S(2)}) collective-permute-start(bf16[1024,384]{1,0:T(8,128)(2,1)S(1)} %get-tuple-element.113), channel_id=1, source_target_pairs={{2,0},{4,2},{6,4},{8,6},{10,8},{12,10},{14,12},{16,14},{18,16},{20... | collective-permute-start | bytes 2359304 | tf_op jit(solution)/shard_map/ppermute | solution.py:20
  336.8 26.2 %copy-start.26 = (f32[768]{0:T(1024)S(1)}, f32[768]{0:T(1024)}, u32[]{:S(2)}) copy-start(f32[768]{0:T(1024)} %param.29) | copy-start | bytes 9220
  339.5 62.8 %all-reduce.16.cloned.1.call-start = ((), (), s32[]{:S(2)}) async-start(), calls=%async_computation.4 | async-start | bytes 6291456 | tf_op jit(solution)/shard_map/psum | solution.py:144
  365.9 6.0 copy-start.2
  366.7 6.8 copy-start.32
  377.8 24.6 %copy-start.27 = (f32[768]{0:T(1024)S(1)}, f32[768]{0:T(1024)}, u32[]{:S(2)}) copy-start(f32[768]{0:T(1024)} %param.35) | copy-start | bytes 9220
  377.8 70.4 %all-reduce.18.cloned.1.call-start = ((), (), s32[]{:S(2)}) async-start(), calls=%async_computation.5 | async-start | bytes 6291456 | tf_op jit(solution)/shard_map/psum | solution.py:159
  406.8 2.6 copy-start.28
  407.6 4.3 slice-start
  409.4 2.6 copy-start.33
  409.4 3.5 slice-start.1
  412.0 5.7 copy-start.8
  423.6 524.6 %all-reduce.20.cloned.1.call-start = ((), (), s32[]{:S(2)}) async-start(), calls=%async_computation.6 | async-start | bytes 3145728 | tf_op jit(solution)/shard_map/psum | solution.py:221
  452.9 2.6 copy-start.18
  455.5 42.6 %copy-start.3 = (f32[1024,768]{1,0:T(8,128)}, f32[1024,768]{1,0:T(8,128)S(1)}, u32[]{:S(2)}) copy-start(f32[1024,768]{1,0:T(8,128)S(1)} %get-tuple-element.92) | copy-start | bytes 9437188
  456.5 37.7 %collective-permute-start.8 = (bf16[1024,384]{1,0:T(8,128)(2,1)S(1)}, bf16[1024,384]{1,0:T(8,128)(2,1)S(1)}, u32[]{:S(2)}, u32[]{:S(2)}) collective-permute-start(bf16[1024,384]{1,0:T(8,128)(2,1)S(1)} %convolution_convert_fusion), channel_id=1, source_target_pairs={{0,4},{2,6},{4,8},{6,10},{8,12},{10,14},{12,16},{14,18},{16,20},{1... | collective-permute-start | bytes 2359304 | tf_op jit(solution)/shard_map/ppermute | solution.py:20
  460.2 36.9 %collective-permute-start.9 = (bf16[1024,384]{1,0:T(8,128)(2,1)S(1)}, bf16[1024,384]{1,0:T(8,128)(2,1)S(1)}, u32[]{:S(2)}, u32[]{:S(2)}) collective-permute-start(bf16[1024,384]{1,0:T(8,128)(2,1)S(1)} %convolution_convert_fusion), channel_id=1, source_target_pairs={{0,2},{2,4},{4,6},{6,8},{8,10},{10,12},{12,14},{14,16},{16,18},{18... | collective-permute-start | bytes 2359304 | tf_op jit(solution)/shard_map/ppermute | solution.py:20
  463.6 35.7 %collective-permute-start.10 = (bf16[1024,384]{1,0:T(8,128)(2,1)S(1)}, bf16[1024,384]{1,0:T(8,128)(2,1)S(1)}, u32[]{:S(2)}, u32[]{:S(2)}) collective-permute-start(bf16[1024,384]{1,0:T(8,128)(2,1)S(1)} %convolution_convert_fusion), channel_id=1, source_target_pairs={{2,0},{4,2},{6,4},{8,6},{10,8},{12,10},{14,12},{16,14},{18,16},{20... | collective-permute-start | bytes 2359304 | tf_op jit(solution)/shard_map/ppermute | solution.py:20
  464.9 35.4 %collective-permute-start.11 = (bf16[1024,384]{1,0:T(8,128)(2,1)S(1)}, bf16[1024,384]{1,0:T(8,128)(2,1)S(1)}, u32[]{:S(2)}, u32[]{:S(2)}) collective-permute-start(bf16[1024,384]{1,0:T(8,128)(2,1)S(1)} %convolution_convert_fusion), channel_id=1, source_target_pairs={{4,0},{6,2},{8,4},{10,6},{12,8},{14,10},{16,12},{18,14},{20,16},{2... | collective-permute-start | bytes 2359304 | tf_op jit(solution)/shard_map/ppermute | solution.py:20
  507.8 2.7 copy-start.7
  509.0 2.7 copy-start.5
  509.0 2.8 copy-start.10
  513.8 2.1 copy-start.12
  517.4 3.5 copy-start.15
  658.7 67.0 %collective-permute-start.12 = (bf16[3,1024,384]{2,1,0:T(8,128)(2,1)S(1)}, bf16[3,1024,384]{2,1,0:T(8,128)(2,1)S(1)}, u32[]{:S(2)}, u32[]{:S(2)}) collective-permute-start(bf16[3,1024,384]{2,1,0:T(8,128)(2,1)S(1)} %copy.213), channel_id=1, source_target_pairs={{4,0},{6,2},{8,4},{10,6},{12,8},{14,10},{16,12},{18,14},{20,16},{2... | collective-permute-start | bytes 7077896 | tf_op jit(solution)/shard_map/ppermute | solution.py:20
  660.2 70.3 %collective-permute-start.13 = (bf16[3,1024,384]{2,1,0:T(8,128)(2,1)S(1)}, bf16[3,1024,384]{2,1,0:T(8,128)(2,1)S(1)}, u32[]{:S(2)}, u32[]{:S(2)}) collective-permute-start(bf16[3,1024,384]{2,1,0:T(8,128)(2,1)S(1)} %copy.214), channel_id=1, source_target_pairs={{2,0},{4,2},{6,4},{8,6},{10,8},{12,10},{14,12},{16,14},{18,16},{20... | collective-permute-start | bytes 7077896 | tf_op jit(solution)/shard_map/ppermute | solution.py:20
  661.5 119.5 %collective-permute-start.14 = (bf16[3,1024,384]{2,1,0:T(8,128)(2,1)S(1)}, bf16[3,1024,384]{2,1,0:T(8,128)(2,1)S(1)}, u32[]{:S(2)}, u32[]{:S(2)}) collective-permute-start(bf16[3,1024,384]{2,1,0:T(8,128)(2,1)S(1)} %copy.215), channel_id=1, source_target_pairs={{0,2},{2,4},{4,6},{6,8},{8,10},{10,12},{12,14},{14,16},{16,18},{18... | collective-permute-start | bytes 7077896 | tf_op jit(solution)/shard_map/ppermute | solution.py:20
  680.4 146.5 %collective-permute-start.15 = (bf16[3,1024,384]{2,1,0:T(8,128)(2,1)S(1)}, bf16[3,1024,384]{2,1,0:T(8,128)(2,1)S(1)}, u32[]{:S(2)}, u32[]{:S(2)}) collective-permute-start(bf16[3,1024,384]{2,1,0:T(8,128)(2,1)S(1)} %copy.216), channel_id=1, source_target_pairs={{0,4},{2,6},{4,8},{6,10},{8,12},{10,14},{12,16},{14,18},{16,20},{1... | collective-permute-start | bytes 7077896 | tf_op jit(solution)/shard_map/ppermute | solution.py:20
  831.9 211.9 %all-reduce.22.cloned.1.call-start = ((), (), s32[]{:S(2)}) async-start(), calls=%async_computation.10 | async-start | bytes 9437184
  843.6 328.7 %reduce-scatter.4.cloned.1.call-start = ((), (), s32[]{:S(2)}) async-start(), calls=%async_computation.7 | async-start | bytes 1253376 | tf_op jit(solution)/shard_map/reduce_scatter | solution.py:228
  847.8 467.6 %reduce-scatter.8.cloned.1.call-start = ((), (), s32[]{:S(2)}) async-start(), calls=%async_computation.9 | async-start | bytes 5013504 | tf_op jit(solution)/shard_map/reduce_scatter | solution.py:230
  855.6 601.2 %reduce-scatter.6.cloned.1.call-start = ((), (), s32[]{:S(2)}) async-start(), calls=%async_computation.8 | async-start | bytes 5013504 | tf_op jit(solution)/shard_map/reduce_scatter | solution.py:229
  947.6 509.2 %copy-start.1 = (bf16[768,1536]{1,0:T(8,128)(2,1)S(1)}, bf16[768,1536]{1,0:T(8,128)(2,1)}, u32[]{:S(2)}) copy-start(bf16[768,1536]{1,0:T(8,128)(2,1)} %param.32) | copy-start | bytes 7077892
  (16 other events, 20.6 us)
Sparse Core Ops, SparseCore 0:
  339.6 23.3 all-reduce.13
  377.9 24.3 all-reduce.15
  423.7 24.3 all-reduce.17
  832.0 24.4 all-reduce.19
  862.1 181.6 all-reduce.21
  1049.7 122.5 reduce-scatter.3
  1178.9 136.5 reduce-scatter.7
  1321.2 135.5 reduce-scatter.5
where the time goes:
time: 1470 us; the launch traced here: 1460 us
  waiting for transfers between devices  932 us (63%)
  local copies, waits for them, and re-layouts  274 us (19%)
  blocking collectives  78.9 us (5%)
  matrix products  63.8 us (4%)
  starting transfers between devices  62.7 us (4%)
  other arithmetic  37.4 us (3%)
  between operations  15.9 us (1%)
    ppermute x16, waiting for transfers between devices, passed_along(): lax.ppermute(value, axis, [(source, source + steps) for source in range(l...  359 us
    reduce_scatter x1, waiting for transfers between devices, body(): lax.psum_scatter(down_weight_grad, 'seq', scatter_dimension=1, tiled=True)  143 us
    reduce_scatter x1, waiting for transfers between devices, body(): lax.psum_scatter(up_weight_grad, 'seq', scatter_dimension=0, tiled=True)  141 us
    reduce_scatter x1, waiting for transfers between devices, body(): lax.psum_scatter(output_weight_grad, 'seq', scatter_dimension=1, tiled=True)  125 us
    scatter x1, local copies, waits for them, and re-layouts, body(): grad_buffer = jnp.zeros((3, span_rows, slot_grads.shape[2]), jnp.bfloat16...  115 us
    unnamed x9, waiting for transfers between devices  91.2 us
    psum x1, blocking collectives, body(): lax.psum((bias_parts[0], bias_parts[2], up_bias_part), 'seq')  78.9 us
    ppermute x16, starting transfers between devices, passed_along(): lax.ppermute(value, axis, [(source, source + steps) for source in range(l...  61.7 us
  transfers between devices with their start and end apart: 24, of which 18 were waited for; matrix products, arithmetic and copies ran while one was open for 4% of the time, Pallas kernels for 0%

commit v1 on v0

v1 whole, which is shorter than its diff:
```python
import functools

import jax
import jax.numpy as jnp
from jax import lax
from jax.experimental import pallas as pl
from jax.experimental.pallas import tpu as pltpu
from jax.sharding import PartitionSpec as P

MESH = pl.DeviceIdType.MESH
HEAD_DIM = 64
CLUSTER = 128
OFFSETS = (0, 1, -1, 2, -2)
SLOT = {offset: slot for slot, offset in enumerate(OFFSETS)}
MEBI = 1 << 20

norm_eps = 1e-12
masked_score = -1e30
root_half = 0.7071067811865476
inv_root_tau = 0.3989422804014327
score_scale = HEAD_DIM ** (-0.5)

F32 = jnp.float32
BF16 = jnp.bfloat16


def doc_lookup(doc_lengths, positions):
    padded = (doc_lengths + CLUSTER - 1) // CLUSTER * CLUSTER
    starts = jnp.cumsum(padded) - padded
    doc_of = jnp.sum((starts[None, :] <= positions[:, None]).astype(jnp.int32), axis=1) - 1
    picked = jnp.arange(starts.shape[0], dtype=jnp.int32)[None, :] == doc_of[:, None]
    slot_start = jnp.sum(jnp.where(picked, starts[None, :], 0), axis=1)
    slot_length = jnp.sum(jnp.where(picked, doc_lengths[None, :], 0), axis=1)
    return (slot_start, slot_length)


def remote(src, dst, send, recv, device):
    return pltpu.make_async_remote_copy(
        src_ref=src, dst_ref=dst, send_sem=send, recv_sem=recv, device_id=device, device_id_type=MESH
    )


def greet(devices):
    barrier = pltpu.get_barrier_semaphore()
    count = 0
    for device, valid in devices:
        def hello(device=device):
            pl.semaphore_signal(barrier, inc=1, device_id=device, device_id_type=MESH)

        if valid is None:
            hello()
            count = count + 1
        else:
            pl.when(valid)(hello)
            count = count + valid.astype(jnp.int32)
    pl.semaphore_wait(barrier, count)


def near(seq, core, blocks):
    out = {}
    for offset in OFFSETS[1:]:
        there = seq + offset
        out[offset] = ((there, core), (there >= 0) & (there < blocks))
    return out


def inner(left, right):
    return lax.dot_general(left, right, (((1,), (0,)), ((), ())), preferred_element_type=F32)


def outer(left, right):
    return lax.dot_general(left, right, (((1,), (1,)), ((), ())), preferred_element_type=F32)


def under(left, right):
    return lax.dot_general(left, right, (((0,), (0,)), ((), ())), preferred_element_type=F32)


def entry_kernel(
    blocks,
    tokens,
    out_grad,
    rel,
    source,
    wq,
    wk,
    wv,
    wo,
    wu,
    wd,
    bq,
    bv,
    bu,
    slot_tokens,
    slot_grad,
    sources,
    wqkv_full,
    wo_full,
    wu_full,
    wd_full,
    bqkv_full,
    bu_full,
    window,
    total,
    picked,
    source_win,
    wsend,
    wrecv,
    wlocal,
    send,
    recv,
    local,
    ssend,
    srecv,
    psend,
    precv,
    plocal,
):
    seq, core = lax.axis_index("seq"), lax.axis_index("head")
    rows, width = window.shape[2], window.shape[3]
    half = rows // 2
    partner = (seq, 1 - core)
    others = near(seq, core, blocks)
    greet([(partner, None)] + [others[offset] for offset in OFFSETS[1:]])

    mine = pl.ds(pl.multiple_of(core * width, width), width)
    arrays = (tokens, out_grad)
    locals_ = []
    for which, array in enumerate(arrays):
        for offset in OFFSETS[1:]:
            device, valid = others[offset]
            slot = SLOT[-offset]
            copy = remote(
                array.at[:, mine], window.at[which, slot], send.at[which, slot], recv.at[which, slot], device
            )
            pl.when(valid)(copy.start)
            if which == 0:
                tiny = remote(source, source_win.at[slot], ssend.at[slot], srecv.at[slot], device)
                pl.when(valid)(tiny.start)
        own = pltpu.make_async_copy(array.at[:, mine], window.at[which, 0], local.at[which])
        own.start()
        locals_.append(own)

    wide, deep = wq.shape[1], wd.shape[0]
    model = wq.shape[0]
    at_core = pl.multiple_of(core * wide, wide)
    at_deep = pl.multiple_of(core * deep, deep)
    pieces = []
    for i, array in enumerate((wq, wk, wv)):
        at = pl.multiple_of(i * model + core * wide, wide)
        pieces.append((array, wqkv_full.at[:, pl.ds(at, wide)]))
    pieces.append((wo, wo_full.at[pl.ds(at_core, wide), :]))
    pieces.append((wu, wu_full.at[:, pl.ds(at_deep, deep)]))
    pieces.append((wd, wd_full.at[pl.ds(at_deep, deep), :]))
    pieces.append((bq, bqkv_full.at[:, pl.ds(at_core, wide)]))
    pieces.append((bv, bqkv_full.at[:, pl.ds(pl.multiple_of(2 * model + core * wide, wide), wide)]))
    pieces.append((bu, bu_full.at[:, pl.ds(at_deep, deep)]))
    moves = []
    for i, (array, place) in enumerate(pieces):
        there = remote(array, place, wsend.at[i], wrecv.at[i], partner)
        here = pltpu.make_async_copy(array, place, wlocal.at[i])
        there.start()
        here.start()
        moves.append((there, here))

    source_win[0] = source[...]
    for offset in OFFSETS[1:]:

        def blank(slot=SLOT[offset]):
            source_win[slot] = jnp.full(source.shape, -1, jnp.int32)

        pl.when(jnp.logical_not(others[offset][1]))(blank)
    tile = 256
    outs = (slot_tokens, slot_grad)
    finals = []
    for which in range(2):
        locals_[which].wait()
        for offset in OFFSETS:
            slot = SLOT[offset]

            def add(which=which, offset=offset, slot=slot):
                if offset != 0:
                    device, _ = others[offset]
                    remote(
                        arrays[which].at[:, mine],
                        window.at[which, slot],
                        send.at[which, slot],
                        recv.at[which, slot],
                        device,
                    ).wait_recv()

                @pl.loop(0, rows // tile)
                def _(step):
                    at = pl.ds(pl.multiple_of(step * tile, tile), tile)
                    wanted = rel[at, :] - offset * rows
                    lanes = lax.broadcasted_iota(jnp.int32, (tile, rows), 1)
                    chosen = jnp.where(lanes == wanted, 1.0, 0.0).astype(BF16)
                    part = inner(chosen, window[which, slot])
                    if offset == 0:
                        total[at, :] = part
                    else:
                        total[at, :] += part

            if offset == 0:
                add()
            else:
                pl.when(others[offset][1])(add)
        picked[which] = total[...].astype(BF16)
        keep = pl.ds(pl.multiple_of(core * half, half), half)
        give = pl.ds(pl.multiple_of((1 - core) * half, half), half)
        there = remote(
            picked.at[which, give], outs[which].at[:, mine], psend.at[which], precv.at[which], partner
        )
        here = pltpu.make_async_copy(picked.at[which, keep], outs[which].at[:, mine], plocal.at[which])
        there.start()
        here.start()
        finals.append((there, here))

    for offset in OFFSETS[1:]:
        device, valid = others[offset]

        def finish(offset=offset, device=device):
            for which in range(2):
                slot = SLOT[-offset]
                remote(
                    arrays[which].at[:, mine],
                    window.at[which, slot],
                    send.at[which, slot],
                    recv.at[which, slot],
                    device,
                ).wait_send()
            slot = SLOT[-offset]
            remote(source, source_win.at[slot], ssend.at[slot], srecv.at[slot], device).wait_send()
            slot = SLOT[offset]
            remote(source, source_win.at[slot], ssend.at[slot], srecv.at[slot], device).wait_recv()

        pl.when(valid)(finish)
    sources[...] = source_win[...]
    for there, here in moves + finals:
        there.wait()
        here.wait()


def entry(mesh, tokens, out_grad, rel, source, wq, wk, wv, wo, wu, wd, bq, bv, bu):
    rows, model = tokens.shape
    width = model // 2
    hidden = 2 * wu.shape[1]
    hbm = pl.BlockSpec(memory_space=pl.ANY)
    vmem = pl.BlockSpec(memory_space=pltpu.VMEM)
    slots = len(OFFSETS)
    dma = pltpu.SemaphoreType.DMA
    return pl.pallas_call(
        functools.partial(entry_kernel, mesh.shape["seq"]),
        out_shape=(
            jax.ShapeDtypeStruct((rows // 2, model), BF16),
            jax.ShapeDtypeStruct((rows // 2, model), BF16),
            jax.ShapeDtypeStruct((slots, 1, rows), jnp.int32),
            jax.ShapeDtypeStruct((model, 3 * model), BF16),
            jax.ShapeDtypeStruct((model, model), BF16),
            jax.ShapeDtypeStruct((model, hidden), BF16),
            jax.ShapeDtypeStruct((hidden, model), BF16),
            jax.ShapeDtypeStruct((1, 3 * model), F32),
            jax.ShapeDtypeStruct((1, hidden), F32),
        ),
        in_specs=[hbm, hbm, vmem, vmem] + [hbm] * 9,
        out_specs=(hbm, hbm, vmem) + (hbm,) * 6,
        scratch_shapes=[
            pltpu.VMEM((2, slots, rows, width), BF16),
            pltpu.VMEM((rows, width), F32),
            pltpu.VMEM((2, rows, width), BF16),
            pltpu.VMEM((slots, 1, rows), jnp.int32),
            dma((9,)),
            dma((9,)),
            dma((9,)),
            dma((2, slots)),
            dma((2, slots)),
            dma((2,)),
            dma((slots,)),
            dma((slots,)),
            dma((2,)),
            dma((2,)),
            dma((2,)),
        ],
        compiler_params=pltpu.CompilerParams(
            collective_id=0, has_side_effects=True, vmem_limit_bytes=40 * MEBI
        ),
    )(tokens, out_grad, rel, source, wq, wk, wv, wo, wu, wd, bq, bv, bu)


def fold_rows(values):
    return jnp.sum(values.reshape(values.shape[0] // 8, 8, values.shape[1]), axis=0)


def layer_kernel(
    chunk,
    x,
    og,
    valid,
    wqkv,
    wo,
    wu,
    wd,
    bqkv,
    bo,
    g1,
    s1,
    bu,
    bd,
    g2,
    s2,
    out_low,
    in_low,
    grads,
    sums,
    qkv,
    ctx,
    prob,
    hat1,
    inv1,
    low1,
    act,
    slope,
    pre_low,
    work,
    flipped,
    dqkv,
    cgrad,
    low2,
    gtile,
    accs,
    gsem,
):
    rows, model = x.shape
    hidden = wu.shape[1]
    clusters = rows // CLUSTER
    pairs = model // 128
    tile = 256
    band = 64

    def at(step, size):
        return pl.ds(pl.multiple_of(step * size, size), size)

    lanes = lax.broadcasted_iota(jnp.int32, (CLUSTER, 128), 1)
    first_f = jnp.where(lanes < HEAD_DIM, 1.0, 0.0)
    first = first_f.astype(BF16)
    second = (1.0 - first_f).astype(BF16)

    def stacked(pair):
        return jnp.concatenate([pair * first, pair * second], axis=0)

    def beside(tall):
        return jnp.concatenate([tall[:CLUSTER], tall[CLUSTER:]], axis=1)

    @pl.loop(0, 3 * model // tile)
    def _(step):
        cols = at(step, tile)
        qkv[:, cols] = (inner(x[...], wqkv[:, cols]) + bqkv[:, cols]).astype(BF16)

    @pl.loop(0, clusters * pairs)
    def _(step):
        cluster, pair = step // pairs, step % pairs
        r = at(cluster, CLUSTER)
        q = qkv[r, at(pair, 128)]
        k = qkv[r, pl.ds(pl.multiple_of(model + pair * 128, 128), 128)]
        v = qkv[r, pl.ds(pl.multiple_of(2 * model + pair * 128, 128), 128)]
        scores = outer(stacked(q), k) * score_scale
        scores = jnp.where(valid[cluster] > 0.5, scores, masked_score)
        top = jnp.max(scores, axis=-1, keepdims=True)
        weight = jnp.exp(scores - top)
        p = weight / jnp.sum(weight, axis=-1, keepdims=True)
        prob[step] = p
        ctx[r, at(pair, 128)] = inner(beside(p.astype(BF16)), stacked(v)).astype(BF16)

    @pl.loop(0, model // tile)
    def _(step):
        cols = at(step, tile)
        hat1[:, cols] = inner(ctx[...], wo[:, cols]) + x[:, cols].astype(F32) + bo[:, cols]

    @pl.loop(0, rows // band)
    def _(step):
        r = at(step, band)
        h = hat1[r, :]
        centered = h - jnp.mean(h, axis=-1, keepdims=True)
        inv = lax.rsqrt(jnp.mean(centered * centered, axis=-1, keepdims=True) + norm_eps)
        hat = centered * inv
        hat1[r, :] = hat
        inv1[r, :] = inv
        low1[r, :] = (hat * g1[...] + s1[...]).astype(BF16)

    @pl.loop(0, hidden // tile)
    def _(step):
        cols = at(step, tile)
        pre = inner(low1[...], wu[:, cols]) + bu[:, cols]
        cdf = 0.5 * (1.0 + lax.erf(pre * root_half))
        act[:, cols] = (pre * cdf).astype(BF16)
        slope[:, cols] = cdf + pre * jnp.exp(-0.5 * pre * pre) * inv_root_tau

    @pl.loop(0, model // tile)
    def _(step):
        cols = at(step, tile)
        norm = hat1[:, cols] * g1[:, cols] + s1[:, cols]
        work[:, cols] = inner(act[...], wd[:, cols]) + norm + bd[:, cols]

    accs[...] = jnp.zeros_like(accs)

    @pl.loop(0, rows // band)
    def _(step):
        r = at(step, band)
        h = work[r, :]
        centered = h - jnp.mean(h, axis=-1, keepdims=True)
        inv = lax.rsqrt(jnp.mean(centered * centered, axis=-1, keepdims=True) + norm_eps)
        hat = centered * inv
        out_low[r, :] = (hat * g2[...] + s2[...]).astype(BF16)
        grad = og[r, :].astype(F32)
        accs[4] += fold_rows(grad * hat)
        accs[5] += fold_rows(grad)
        scaled = grad * g2[...]
        back = inv * (
            scaled
            - jnp.mean(scaled, axis=-1, keepdims=True)
            - hat * jnp.mean(scaled * hat, axis=-1, keepdims=True)
        )
        accs[3] += fold_rows(back)
        work[r, :] = back
        low2[r, :] = back.astype(BF16)

    def flip(source):
        @pl.loop(0, model // 128)
        def _(step):
            flipped[at(step, 128), :] = source[:, at(step, 128)].T

    half_rows = model // 2
    chunks = half_rows // chunk

    def product_tiles(right, width, places, count):
        def moves(index, slot):
            m, n = index // count, index % count
            for piece, (part, start, size) in enumerate(places(n)):
                yield pltpu.make_async_copy(
                    gtile.at[slot, :, :, pl.ds(piece * size, size)] if size != width
                    else gtile.at[slot, :, :, pl.ds(0, width)],
                    grads.at[part, pl.ds(m * chunks, chunks), :, pl.ds(start, size)],
                    gsem.at[slot, piece],
                )

        total = 2 * count

        @pl.loop(0, total)
        def _(index):
            slot = index % 2
            m, n = index // count, index % count

            @pl.when(index >= 2)
            def _():
                for move in moves(index - 2, slot):
                    move.wait()

            value = inner(flipped[at(m, half_rows), :], right[:, at(n, width)])
            gtile[slot, :, :, pl.ds(0, width)] = value.reshape(chunks, chunk, width).astype(BF16)
            for move in moves(index, slot):
                move.start()

        for index in range(max(total - 2, 0), total):
            for move in moves(index, index % 2):
                move.wait()

    part_q = model // 2
    part_h = hidden // 2
    wide = 512

    def square(which):
        def places(n):
            return [(0, which * part_q, part_q), (1, which * part_q, part_q)]

        return places

    def long(base):
        per_part = part_h // wide

        def places(n):
            part, inside = n // per_part, n % per_part
            return [(part, pl.multiple_of(base + inside * wide, 128), wide)]

        return places

    flip(low2)
    product_tiles(act, wide, long(4 * part_q + part_h), hidden // wide)

    @pl.loop(0, hidden // tile)
    def _(step):
        cols = at(step, tile)
        back = outer(low2[...], wd[cols, :]) * slope[:, cols]
        back = back.astype(BF16)
        pre_low[:, cols] = back
        sums[:, pl.ds(pl.multiple_of(2 * model + step * tile, tile), tile)] = jnp.sum(
            back.astype(F32), axis=0, keepdims=True
        )

    flip(low1)
    product_tiles(pre_low, wide, long(4 * part_q), hidden // wide)

    @pl.loop(0, model // tile)
    def _(step):
        cols = at(step, tile)
        work[:, cols] += outer(pre_low[...], wu[cols, :])

    @pl.loop(0, rows // band)
    def _(step):
        r = at(step, band)
        grad = work[r, :]
        hat = hat1[r, :]
        accs[1] += fold_rows(grad * hat)
        accs[2] += fold_rows(grad)
        scaled = grad * g1[...]
        back = inv1[r, :] * (
            scaled
            - jnp.mean(scaled, axis=-1, keepdims=True)
            - hat * jnp.mean(scaled * hat, axis=-1, keepdims=True)
        )
        accs[0] += fold_rows(back)
        work[r, :] = back
        low2[r, :] = back.astype(BF16)

    flip(low2)
    product_tiles(ctx, model, square(3), 1)

    @pl.loop(0, model // tile)
    def _(step):
        cols = at(step, tile)
        cgrad[:, cols] = outer(low2[...], wo[cols, :]).astype(BF16)

    @pl.loop(0, clusters * pairs)
    def _(step):
        cluster, pair = step // pairs, step % pairs
        r = at(cluster, CLUSTER)
        at_q = at(pair, 128)
        at_k = pl.ds(pl.multiple_of(model + pair * 128, 128), 128)
        at_v = pl.ds(pl.multiple_of(2 * model + pair * 128, 128), 128)
        q, k, v = qkv[r, at_q], qkv[r, at_k], qkv[r, at_v]
        p = prob[step]
        dctx = stacked(cgrad[r, at_q])
        dprob = outer(dctx, v)
        dscore = (p * (dprob - jnp.sum(p * dprob, axis=-1, keepdims=True))).astype(BF16)
        dqkv[r, at_q] = (inner(beside(dscore), stacked(k)) * score_scale).astype(BF16)
        dqkv[r, at_k] = (under(dscore, stacked(q)) * score_scale).astype(BF16)
        dqkv[r, at_v] = under(p.astype(BF16), dctx).astype(BF16)

    flip(x)
    for which in range(3):
        product_tiles(dqkv.at[:, pl.ds(which * model, model)], model, square(which), 1)

    for which in range(2):
        @pl.loop(0, model // tile)
        def _(step, which=which):
            value = dqkv[:, pl.ds(pl.multiple_of(2 * which * model + step * tile, tile), tile)]
            sums[:, pl.ds(pl.multiple_of(which * model + step * tile, tile), tile)] = jnp.sum(
                value.astype(F32), axis=0, keepdims=True
            )

    @pl.loop(0, model // tile)
    def _(step):
        cols = at(step, tile)
        in_low[:, cols] = (work[:, cols] + outer(dqkv[...], wqkv[cols, :])).astype(BF16)

    for i in range(6):
        sums[:, pl.ds(2 * model + hidden + i * model, model)] = jnp.sum(accs[i], axis=0, keepdims=True)


def layer(chunk, x, og, valid, wqkv, wo, wu, wd, bqkv, bo, g1, s1, bu, bd, g2, s2):
    rows, model = x.shape
    hidden = wu.shape[1]
    hbm = pl.BlockSpec(memory_space=pl.ANY)
    vmem = pl.BlockSpec(memory_space=pltpu.VMEM)
    part = 2 * model + hidden
    steps = rows // CLUSTER * (model // 128)
    total = 8 * model + hidden
    return pl.pallas_call(
        functools.partial(layer_kernel, chunk),
        out_shape=(
            jax.ShapeDtypeStruct((rows, model), BF16),
            jax.ShapeDtypeStruct((rows, model), BF16),
            jax.ShapeDtypeStruct((2, model // chunk, chunk, part), BF16),
            jax.ShapeDtypeStruct((1, total), F32),
        ),
        in_specs=[vmem] * 15,
        out_specs=(vmem, vmem, hbm, vmem),
        scratch_shapes=[
            pltpu.VMEM((rows, 3 * model), BF16),
            pltpu.VMEM((rows, model), BF16),
            pltpu.VMEM((steps, 2 * CLUSTER, CLUSTER), F32),
            pltpu.VMEM((rows, model), F32),
            pltpu.VMEM((rows, 1), F32),
            pltpu.VMEM((rows, model), BF16),
            pltpu.VMEM((rows, hidden), BF16),
            pltpu.VMEM((rows, hidden), F32),
            pltpu.VMEM((rows, hidden), BF16),
            pltpu.VMEM((rows, model), F32),
            pltpu.VMEM((model, rows), BF16),
            pltpu.VMEM((rows, 3 * model), BF16),
            pltpu.VMEM((rows, model), BF16),
            pltpu.VMEM((rows, model), BF16),
            pltpu.VMEM((2, model // 2 // chunk, chunk, model), BF16),
            pltpu.VMEM((6, 8, model), F32),
            pltpu.SemaphoreType.DMA((2, 2)),
        ],
        compiler_params=pltpu.CompilerParams(vmem_limit_bytes=60 * MEBI),
    )(x, og, valid, wqkv, wo, wu, wd, bqkv, bo, g1, s1, bu, bd, g2, s2)


def exit_kernel(blocks, reduce, *refs):
    if reduce:
        (out_low, in_low, sources, grads, sums, out_home, in_home, grad_sum, sums_sum, *scratch) = refs
        (window, home, wsend, wrecv, csend, crecv, clocal, hsend, hrecv, hlocal, *scratch) = scratch
        (mine_g, from_core, got, gsend, grecv, glocal, rsend, rrecv, vrecv, vsend, vsem) = scratch
    else:
        (out_low, in_low, sources, out_home, in_home, *scratch) = refs
        (window, home, wsend, wrecv, csend, crecv, clocal, hsend, hrecv, hlocal) = scratch
    seq, core = lax.axis_index("seq"), lax.axis_index("head")
    rows, width = window.shape[2], window.shape[3]
    half = rows // 2
    partner = (seq, 1 - core)
    others = near(seq, core, blocks)
    bits = max(blocks.bit_length() - 1, 0)
    greetings = [(partner, None)] + [others[offset] for offset in OFFSETS[1:]]

    def across(bit):
        mask = 1 << bit
        return (seq + mask - 2 * mask * ((seq // mask) % 2), core)

    if reduce:
        greetings += [(across(bit), None) for bit in range(2, bits)]
    greet(greetings)

    mine = pl.ds(pl.multiple_of(core * width, width), width)
    theirs = pl.ds(pl.multiple_of((1 - core) * width, width), width)
    keep = pl.ds(pl.multiple_of(core * half, half), half)
    arrays = (out_low, in_low)
    firsts = []
    for which, array in enumerate(arrays):
        there = remote(
            array.at[:, theirs], window.at[which, 0, keep], csend.at[which], crecv.at[which], partner
        )
        here = pltpu.make_async_copy(array.at[:, mine], window.at[which, 0, keep], clocal.at[which])
        there.start()
        here.start()
        firsts.append((there, here))

    if reduce:
        parts = 2
        span = mine_g.shape[3] // parts
        core_moves = []
        for part in range(parts):
            cols = pl.ds(part * span, span)
            there = remote(
                grads.at[1 - core, :, :, cols], from_core.at[:, :, cols], gsend.at[part], grecv.at[part], partner
            )
            here = pltpu.make_async_copy(grads.at[core, :, :, cols], mine_g.at[0, :, :, cols], glocal.at[part])
            there.start()
            here.start()
            core_moves.append((there, here))

    def spread(which):
        for offset in OFFSETS[1:]:
            device, valid = others[offset]
            slot = SLOT[-offset]
            pl.when(valid)(
                remote(
                    window.at[which, 0], window.at[which, slot], wsend.at[which, slot], wrecv.at[which, slot], device
                ).start
            )

    for which in range(2):
        there, here = firsts[which]
        there.wait()
        here.wait()
        spread(which)

    def reduce_start(part, level):
        cols = pl.ds(part * span, span)
        order = orders[part]
        bit = order[level]
        own = (seq // (1 << bit)) % 2
        left = sorted(set(range(bits)) - set(order[:level]))
        low = 1 << left.index(bit)
        high = (1 << len(left)) // (2 * low)
        outs = []
        for top in range(high):
            src = mine_g.at[level % 2, pl.ds(pl.multiple_of((top * 2 + 1 - own) * low, low), low), :, cols]
            dst = got.at[pl.ds(base[level] + top * low, low), :, cols]
            outs.append(remote(src, dst, rsend.at[part, level, top], rrecv.at[part, level, top], across(bit)))
        return outs, own, low, high, cols

    def reduce_finish(part, level, state):
        outs, own, low, high, cols = state
        for copy in outs:
            copy.wait()
        for top in range(high):
            @pl.loop(0, low)
            def _(inside):
                held = mine_g[level % 2, (top * 2 + own) * low + inside, :, cols].astype(F32)
                other = got[base[level] + top * low + inside, :, cols].astype(F32)
                value = held + other
                if level == bits - 1:
                    grad_sum[:, cols] = value
                else:
                    mine_g[(level + 1) % 2, top * low + inside, :, cols] = value.astype(BF16)

    def pick(which):
        tile = 256
        for offset in OFFSETS:
            slot = SLOT[offset]

            def add(offset=offset, slot=slot):
                if offset != 0:
                    device, _ = others[offset]
                    remote(
                        window.at[which, 0],
                        window.at[which, slot],
                        wsend.at[which, slot],
                        wrecv.at[which, slot],
                        device,
                    ).wait_recv()

                @pl.loop(0, rows // tile)
                def _(step):
                    at = pl.ds(pl.multiple_of(step * tile, tile), tile)
                    places = lax.broadcasted_iota(jnp.int32, (tile, rows), 0) + (step * tile + seq * rows)
                    chosen = jnp.where(sources[slot] == places, 1.0, 0.0).astype(BF16)
                    part = inner(chosen, window[which, slot]).astype(BF16)
                    if offset == 0:
                        home[which, at, :] = part
                    else:
                        home[which, at, :] += part

            if offset == 0:
                add()
            else:
                pl.when(others[offset][1])(add)
        target = (out_home, in_home)[which]
        there = remote(home.at[which], target.at[:, mine], hsend.at[which], hrecv.at[which], partner)
        here = pltpu.make_async_copy(home.at[which], target.at[:, mine], hlocal.at[which])
        there.start()
        here.start()
        return there, here

    lasts = []
    if not reduce:
        lasts = [pick(0), pick(1)]
    else:
        orders = ([0, 1] + list(range(bits - 1, 1, -1)), [1, 0] + list(range(bits - 1, 1, -1)))
        base, count = [], 0
        for level in range(bits):
            base.append(count)
            count += blocks >> (level + 1)

        def sum_level(level):
            device = partner if level == 0 else across(level - 1)
            return remote(vsend.at[level], vrecv.at[level], vsem.at[0, level], vsem.at[1, level], device)

        def sum_start(level):
            if level == 0:
                vsend[0] = sums[...]
            sum_level(level).start()

        def sum_finish(level):
            sum_level(level).wait()
            value = vsend[level] + vrecv[level]
            if level == bits:
                sums_sum[...] = value
            else:
                vsend[level + 1] = value

        sum_start(0)
        states = [None] * parts
        for part in range(parts):
            there, here = core_moves[part]
            there.wait()
            here.wait()
            cols = pl.ds(part * span, span)

            @pl.loop(0, blocks)
            def _(inside):
                value = mine_g[0, inside, :, cols].astype(F32) + from_core[inside, :, cols].astype(F32)
                mine_g[0, inside, :, cols] = value.astype(BF16)

            states[part] = reduce_start(part, 0)
            for copy in states[part][0]:
                copy.start()
        sum_finish(0)
        sum_start(1)
        lasts.append(pick(0))
        for level in range(bits):
            for part in range(parts):
                reduce_finish(part, level, states[part])
                if level + 1 < bits:
                    states[part] = reduce_start(part, level + 1)
                    for copy in states[part][0]:
                        copy.start()
            sum_finish(level + 1)
            if level + 1 < bits:
                sum_start(level + 2)
            if level == 1:
                lasts.append(pick(1))
        if bits < 2:
            lasts.append(pick(1))

    for offset in OFFSETS[1:]:
        device, valid = others[offset]
        slot = SLOT[-offset]

        def finish(device=device, slot=slot):
            for which in range(2):
                remote(
                    window.at[which, 0], window.at[which, slot], wsend.at[which, slot], wrecv.at[which, slot], device
                ).wait_send()

        pl.when(valid)(finish)
    for there, here in lasts:
        there.wait()
        here.wait()


def leave(mesh, reduce, out_low, in_low, sources, grads, sums):
    half, model = out_low.shape
    rows, width = 2 * half, model // 2
    blocks = mesh.shape["seq"]
    slots = len(OFFSETS)
    hbm = pl.BlockSpec(memory_space=pl.ANY)
    vmem = pl.BlockSpec(memory_space=pltpu.VMEM)
    dma = pltpu.SemaphoreType.DMA
    out_shape = [jax.ShapeDtypeStruct((rows, model), BF16)] * 2
    out_specs = [hbm, hbm]
    in_specs = [hbm, hbm, vmem]
    args = [out_low, in_low, sources]
    scratch = [
        pltpu.VMEM((2, slots, rows, width), BF16),
        pltpu.VMEM((2, rows, width), BF16),
        dma((2, slots)),
        dma((2, slots)),
        dma((2,)),
        dma((2,)),
        dma((2,)),
        dma((2,)),
        dma((2,)),
        dma((2,)),
    ]
    if reduce:
        _, chunks, chunk, span = grads.shape
        bits = blocks.bit_length() - 1
        args += [grads, sums]
        in_specs += [hbm, vmem]
        out_shape += [jax.ShapeDtypeStruct((chunk, span), F32), jax.ShapeDtypeStruct(sums.shape, F32)]
        out_specs += [vmem, vmem]
        scratch += [
            pltpu.VMEM((2, blocks, chunk, span), BF16),
            pltpu.VMEM((blocks, chunk, span), BF16),
            pltpu.VMEM((blocks, chunk, span), BF16),
            dma((2,)),
            dma((2,)),
            dma((2,)),
            dma((2, bits, blocks // 2)),
            dma((2, bits, blocks // 2)),
            pltpu.VMEM((bits + 1,) + sums.shape, F32),
            pltpu.VMEM((bits + 1,) + sums.shape, F32),
            dma((2, bits + 1)),
        ]
    return pl.pallas_call(
        functools.partial(exit_kernel, blocks, reduce),
        out_shape=tuple(out_shape),
        in_specs=in_specs,
        out_specs=tuple(out_specs),
        scratch_shapes=scratch,
        compiler_params=pltpu.CompilerParams(
            collective_id=1, has_side_effects=True, vmem_limit_bytes=60 * MEBI
        ),
    )(*args)


def body(
    mesh,
    tokens,
    out_grad,
    doc_lengths,
    cluster_perm,
    query_weight,
    query_bias,
    key_weight,
    value_weight,
    value_bias,
    output_weight,
    output_bias,
    first_gain,
    first_shift,
    up_weight,
    up_bias,
    down_weight,
    down_bias,
    second_gain,
    second_shift,
):
    rows, model = tokens.shape
    half = rows // 2
    hidden = 2 * up_weight.shape[1]
    blocks = mesh.shape["seq"]
    seq, core = lax.axis_index("seq"), lax.axis_index("head")
    positions = seq * rows + jnp.arange(rows, dtype=jnp.int32)
    slot_start, slot_length = doc_lookup(doc_lengths, positions)
    source = slot_start + cluster_perm
    valid = (cluster_perm < slot_length).astype(F32).reshape(2, half // CLUSTER, 1, CLUSTER)
    valid = lax.dynamic_index_in_dim(valid, core, 0, keepdims=False)

    def row(v):
        return v.reshape(1, -1)

    x, og, sources, wqkv, wo, wu, wd, bqkv, bu = entry(
        mesh,
        tokens,
        out_grad,
        (source - seq * rows).reshape(rows, 1),
        row(source),
        query_weight,
        key_weight,
        value_weight,
        output_weight,
        up_weight,
        down_weight,
        row(query_bias),
        row(value_bias),
        row(up_bias),
    )
    no_key = (jnp.arange(3 * model) // model != 1)[None, :]
    bqkv = jnp.where(no_key, bqkv, 0.0)
    chunk = model // blocks
    reduce = chunk % 16 == 0 and blocks >= 4 and blocks & (blocks - 1) == 0
    out_low, in_low, grads, sums = layer(
        chunk if reduce else 48,
        x,
        og,
        valid,
        wqkv,
        wo,
        wu,
        wd,
        bqkv,
        row(output_bias),
        row(first_gain),
        row(first_shift),
        bu,
        row(down_bias),
        row(second_gain),
        row(second_shift),
    )
    if reduce:
        out_home, in_home, grad_sum, sums = leave(mesh, True, out_low, in_low, sources, grads, sums)
    else:
        out_home, in_home = leave(mesh, False, out_low, in_low, sources, None, None)
        sums = lax.psum(sums, ("seq", "head"))
        grads = grads.reshape(2, model, -1)
        grads = lax.psum_scatter(grads.astype(F32), "head", scatter_dimension=0, tiled=True)[0]
        grad_sum = lax.psum_scatter(grads, "seq", scatter_dimension=0, tiled=True)
    part_q, part_h = model // 2, hidden // 2
    cuts = [part_q * i for i in range(5)] + [4 * part_q + part_h, 4 * part_q + 2 * part_h]
    dwq, dwk, dwv, dwo, dwu, dwd = (grad_sum[:, a:b] for a, b in zip(cuts[:-1], cuts[1:]))
    sums = sums[0]

    def mine(start, size):
        return lax.dynamic_slice(sums, (start + core * size,), (size,))

    def block(index):
        return lax.dynamic_slice(sums, (2 * model + hidden + index * model + seq * chunk,), (chunk,))

    return (
        out_home.astype(F32),
        in_home.astype(F32),
        dwq,
        mine(0, part_q),
        dwk,
        dwv,
        mine(model, part_q),
        dwo.T,
        block(0),
        block(1),
        block(2),
        dwu,
        mine(2 * model, part_h),
        dwd.T,
        block(3),
        block(4),
        block(5),
    )


def solution(mesh):
    placed = (
        P("seq", None),
        P("seq", None),
        P(),
        P("seq"),
        P(None, "head"),
        P("head"),
        P(None, "head"),
        P(None, "head"),
        P("head"),
        P("head", None),
        P(),
        P(),
        P(),
        P(None, "head"),
        P("head"),
        P("head", None),
        P(),
        P(),
        P(),
    )
    return jax.shard_map(
        functools.partial(body, mesh),
        mesh=mesh,
        in_specs=placed,
        out_specs=(
            P("seq", None),
            P("seq", None),
            P("seq", "head"),
            P("head"),
            P("seq", "head"),
            P("seq", "head"),
            P("head"),
            P("head", "seq"),
            P("seq"),
            P("seq"),
            P("seq"),
            P("seq", "head"),
            P("head"),
            P("head", "seq"),
            P("seq"),
            P("seq"),
            P("seq"),
        ),
        check_vma=False,
    )
```

time: 1470 us -> 454 us (0.31)
  waiting for transfers between devices: 932 us -> 0 us
  Pallas kernels: 0 us -> 418 us
  local copies, waits for them, and re-layouts: 274 us -> 26.3 us
  blocking collectives: 78.9 us -> 0 us
  matrix products: 63.8 us -> 0 us
  starting transfers between devices: 62.7 us -> 0 us
  other arithmetic: 37.4 us -> 9.01 us
  between operations: 15.9 us -> 0.78 us
    pallas_call x0 -> x3, Pallas kernels: none -> 418 us  [the longest x1 227 us: leave(): pl.pallas_call(functools.partial(exit_kernel, blocks, reduce), out_shape=...]
    reduce_scatter x3 -> x0, waiting for transfers between devices: 410 us -> none  [the longest x1 143 us: body(): lax.psum_scatter(down_weight_grad, 'seq', scatter_dimension=1, tiled=True)]
    ppermute x16 -> x0, waiting for transfers between devices: 359 us -> none  [passed_along(): lax.ppermute(value, axis, [(source, source + steps) for source in range(l...]
    scatter x2 -> x0, local copies, waits for them, and re-layouts: 123 us -> none  [the longest x1 115 us: body(): grad_buffer = jnp.zeros((3, span_rows, slot_grads.shape[2]), jnp.bfloat16...]
    unnamed x9 -> x0, waiting for transfers between devices: 91.2 us -> none
    psum x1 -> x0, blocking collectives: 78.9 us -> none  [body(): lax.psum((bias_parts[0], bias_parts[2], up_bias_part), 'seq')]
    psum x4 -> x0, waiting for transfers between devices: 72 us -> none  [the longest x1 24.5 us: body(): first_grad = lax.psum(outer_cols(pre_grad, up_weight), 'head') + summed_grad]
    dot_general x18 -> x0, matrix products: 63.8 us -> none  [the longest x3 19.8 us: inner_rows(): lax.dot_general(left, right, (((0,), (0,)), ((), ())), preferred_element_...]
  transfers between devices with their start and end apart: 24 -> 0, of which waited for: 18 -> 0; matrix products, arithmetic and copies ran while one was open for 4% -> 0% of each run, Pallas kernels for 0% -> 0%
where the time goes in v1:
time: 454 us
  Pallas kernels  418 us (92%)
  local copies, waits for them, and re-layouts  26.3 us (6%)
  other arithmetic  9.01 us (2%)
    pallas_call x1, Pallas kernels, leave(): pl.pallas_call(functools.partial(exit_kernel, blocks, reduce), out_shape=...  227 us
    pallas_call x1, Pallas kernels, entry(): pl.pallas_call(functools.partial(entry_kernel, mesh.shape['seq']), out_sh...  105 us
    pallas_call x1, Pallas kernels, layer(): pl.pallas_call(functools.partial(layer_kernel, chunk), out_shape=(jax.Sha...  85.2 us
    unnamed x44, local copies, waits for them, and re-layouts  14.4 us

profile of v1, /device:TPU:0, one launch (start us, length us, event | category | flops | bytes accessed | tf_op | source)
XLA Modules:
  0.0 453.6 jit_solution(13625990838507771086)
XLA Ops:
  0.7 0.7 fusion.9
  1.3 0.2 reduce-window.9
  1.5 0.7 bitcast_subtract_fusion
  2.2 0.1 convert_reduce_fusion
  2.3 0.8 select_reduce_fusion
  3.1 0.7 broadcast_subtract_fusion
  3.8 0.2 copy.37.rel
  4.0 0.7 reshape.160.bu
  4.7 0.7 reshape.158.bq
  5.4 0.7 reshape.159.bv
  6.1 1.7 copy-done
  7.7 1.7 copy-done.1
  9.4 1.4 copy-done.2
  10.8 1.4 copy-done.3
  12.2 1.1 copy-done.7
  13.3 1.1 copy-done.8
  14.3 1.1 copy-done.9
  15.4 1.1 copy-done.10
  16.5 0.0 copy-start.19
  16.5 0.0 copy-start.20
  16.5 0.0 copy-start.21
  16.5 105.0 %shard_map.314 = (bf16[512,768]{1,0:T(8,128)(2,1)S(1)}, bf16[512,768]{1,0:T(8,128)(2,1)S(1)}, s32[5,1,1024]{2,1,0:T(1,128)S(1)}, bf16[768,2304]{1,0:T(8,128)(2,1...) custom-call(bf16[1024,768]{1,0:T(8,128)(2,1)S(1)} %copy-done.2, ...), custom_call_target="tpu_custom_call" | custom-call | tf_op jit(solution)/shard_map/pallas_call | solution.py:252
  121.5 0.0 copy-start.4
  121.5 1.0 copy-done.4
  122.5 0.9 copy-done.5
  123.4 0.9 copy-done.6
  124.3 0.6 copy-done.11
  124.9 0.6 copy-done.12
  125.5 0.6 compare_select_fusion.bqkv
  126.1 0.0 copy-done.15
  126.1 0.6 constant_dynamic-slice_fusion.7
  126.7 0.0 copy-done.16
  126.7 0.6 reshape.163.bo
  127.3 0.6 reshape.164.g1
  127.9 0.6 reshape.165.s1
  128.5 0.6 reshape.166.bd
  129.1 0.6 reshape.167.g2
  129.6 0.0 copy-done.21
  129.6 0.6 reshape.168.s2
  130.2 85.2 %shard_map.315 = (bf16[512,768]{1,0:T(8,128)(2,1)}, bf16[512,768]{1,0:T(8,128)(2,1)}, bf16[2,16,48,4608]{3,2,1,0:T(8,128)(2,1)}, f32[1,9216]{1,0:T(1,128)}) custom-call(bf16[512,768]{1,0:T(8,128)(2,1)} %copy-done.5, bf16[512,768]{1,0:T(8,128)(2,1)} %copy-done.6, f32[4,1,128]{2,1,0:T(1,128)} %bitcast.27, bf16[768,2304]{1,0:T(8,128)(2,1)} %get-tuple-element.36.wqkv, ...), custom_call_target="tpu_custom_call" | custom-call | tf_op jit(solution)/shard_map/pallas_call | solution.py:577
  215.5 227.3 %shard_map.316 = (bf16[1024,768]{1,0:T(8,128)(2,1)}, bf16[1024,768]{1,0:T(8,128)(2,1)}, f32[48,4608]{1,0:T(8,128)}, f32[1,9216]{1,0:T(1,128)}) custom-call(bf16[512,768]{1,0:T(8,128)(2,1)} %get-tuple-element.42.refs_0_, bf16[512,768]{1,0:T(8,128)(2,1)} %get-tuple-element.43.refs_1_, s32[5,1,1024]{2,1,0:T(1,128)} %copy-done.11, ...), custom_call_target="tpu_custom_call" | custom-call | tf_op jit(solution)/shard_map/pallas_call | solution.py:867
  442.8 3.4 convert_element_type.11
  446.2 1.9 convert_element_type.12
  448.1 0.8 slice_bitcast_fusion
  449.0 0.7 slice_bitcast_fusion.1
  449.7 1.3 fusion.2
  451.0 1.3 fusion.1
  452.3 1.3 dynamic-slice_reduce_fusion
  (27 shorter events, 0.1 us)
Async XLA Ops:
  6.1 1.7 copy-start
  7.7 1.7 copy-start.1
  9.4 1.4 copy-start.2
  10.8 1.4 copy-start.3
  12.2 1.1 copy-start.7
  13.3 1.1 copy-start.8
  14.3 1.1 copy-start.9
  15.4 1.1 copy-start.10
  16.5 109.7 %copy-start.15 = (s32[1024]{0:T(1024)S(1)}, s32[1024]{0:T(1024)}, u32[]{:S(2)}) copy-start(s32[1024]{0:T(1024)} %param.22) | copy-start | bytes 12292
  16.5 110.2 %copy-start.16 = (f32[768]{0:T(1024)S(1)}, f32[768]{0:T(1024)}, u32[]{:S(2)}) copy-start(f32[768]{0:T(1024)} %param.29) | copy-start | bytes 9220
  16.5 110.8 %copy-start.17 = (f32[768]{0:T(1024)S(1)}, f32[768]{0:T(1024)}, u32[]{:S(2)}) copy-start(f32[768]{0:T(1024)} %param.30) | copy-start | bytes 9220
  16.5 111.4 %copy-start.18 = (f32[768]{0:T(1024)S(1)}, f32[768]{0:T(1024)}, u32[]{:S(2)}) copy-start(f32[768]{0:T(1024)} %param.31) | copy-start | bytes 9220
  16.5 112.0 %copy-start.19 = (f32[768]{0:T(1024)S(1)}, f32[768]{0:T(1024)}, u32[]{:S(2)}) copy-start(f32[768]{0:T(1024)} %param.35) | copy-start | bytes 9220
  16.5 112.6 %copy-start.20 = (f32[768]{0:T(1024)S(1)}, f32[768]{0:T(1024)}, u32[]{:S(2)}) copy-start(f32[768]{0:T(1024)} %param.36) | copy-start | bytes 9220
  16.5 113.1 %copy-start.21 = (f32[768]{0:T(1024)S(1)}, f32[768]{0:T(1024)}, u32[]{:S(2)}) copy-start(f32[768]{0:T(1024)} %param.37) | copy-start | bytes 9220
  121.5 1.0 copy-start.4
  122.5 0.9 copy-start.5
  123.4 0.9 copy-start.6
  124.3 0.6 copy-start.11
  124.9 0.6 copy-start.12
  442.8 3.4 copy-start.13
  446.2 1.9 copy-start.14

commit v2 on v1

--- a/solution.py
+++ b/solution.py
@@ -876,6 +876,794 @@
     )(*args)
 
 
+FROM_X, FROM_Y, FROM_Z, FROM_LAST, RELAY = range(5)
+OWN = -1
+EXCHANGES = 4
+CHUNKS = 2
+GROUPS = 3
+PARTS = 2
+BITS = 4
+
+
+def whole_kernel(
+    blocks,
+    tokens,
+    out_grad,
+    rel,
+    source,
+    valid,
+    wq,
+    wk,
+    wv,
+    wo_half,
+    wu_half,
+    wd_half,
+    bq,
+    bv,
+    bu_half,
+    bo,
+    g1,
+    s1,
+    bd,
+    g2,
+    s2,
+    out_home,
+    in_home,
+    grad_sum,
+    sums_sum,
+    win,
+    wqkv,
+    wo,
+    wu,
+    wd,
+    bqkv,
+    bu,
+    stage,
+    picked,
+    block,
+    sources,
+    x,
+    og,
+    qkv,
+    ctx,
+    prob,
+    hat1,
+    inv1,
+    low1,
+    act,
+    slope,
+    work,
+    flipped,
+    flipped_x,
+    low2,
+    in_low,
+    accs,
+    mine_g,
+    from_core,
+    give,
+    got0,
+    got1,
+    got2,
+    got3,
+    vsend,
+    vrecv,
+    wsend,
+    wrecv,
+    wlocal,
+    xsend,
+    xrecv,
+    ssend,
+    srecv,
+    ssem,
+    psend,
+    precv,
+    plocal,
+    hsend,
+    hrecv,
+    hlocal,
+    gsend,
+    grecv,
+    rsend,
+    rrecv,
+    vsem,
+    credit,
+):
+    seq, core = lax.axis_index("seq"), lax.axis_index("head")
+    px, py = seq % 2, (seq // 2) % 2
+    rows, width = tokens.shape[0], picked.shape[2]
+    half, model = x.shape
+    hidden = wu.shape[1]
+    clusters = half // CLUSTER
+    pairs = model // 128
+    part_rows = rows // CHUNKS
+    tile = 256
+    band = 64
+
+    partner = (seq, 1 - core)
+    x_next = seq + 1 - 2 * px
+    y_next = seq + 2 - 4 * py
+    z_to = seq + 4 - 8 * py
+    z_from = seq - 4 + 8 * py
+    to_ok = (z_to >= 0) & (z_to < blocks)
+    from_ok = (z_from >= 0) & (z_from < blocks)
+    level_chip = px == py
+    off_chip = px != py
+    last_next = x_next + core * (y_next - x_next)
+    relay_send = (core == 1) & off_chip & from_ok
+    relay_recv = (core == 1) & off_chip & to_ok
+    later_ok = off_chip & (((core == 0) & from_ok) | ((core == 1) & to_ok))
+    last_ok = off_chip | from_ok
+    offsets = {
+        OWN: 0,
+        FROM_X: 1 - 2 * px,
+        FROM_Y: 2 - 4 * py,
+        FROM_Z: 4 * py - 2,
+        FROM_LAST: 2 * px - 1,
+    }
+    arrived = {OWN: None, FROM_X: None, FROM_Y: None, FROM_Z: from_ok, FROM_LAST: last_ok}
+    others = near(seq, core, blocks)
+
+    def across(bit):
+        mask = 1 << bit
+        return (seq + mask - 2 * mask * ((seq // mask) % 2), core)
+
+    greetings = [(partner, None), ((x_next, core), None), ((y_next, core), None)]
+    greetings += [((z_to, core), to_ok), ((z_from, core), from_ok)]
+    greetings += [others[offset] for offset in OFFSETS[1:]]
+    greetings += [(across(bit), None) for bit in range(BITS)]
+    greet(greetings)
+
+    def at(step, size):
+        return pl.ds(pl.multiple_of(step * size, size), size)
+
+    def when(condition, action):
+        if condition is None:
+            action()
+        else:
+            pl.when(condition)(action)
+
+    mine = at(core, width)
+    theirs = at(1 - core, width)
+    keep = at(core, half)
+    other_rows = at(1 - core, half)
+
+    def piece(chunk):
+        return pl.ds(chunk * part_rows, part_rows)
+
+    def own_rows(e, chunk):
+        if e < 2:
+            return (tokens, out_grad)[e].at[piece(chunk), mine]
+        return block.at[e - 2, piece(chunk)]
+
+    def hop(e, kind, chunk, src, there):
+        return remote(
+            src,
+            win.at[e, kind, piece(chunk)],
+            xsend.at[e, kind, chunk],
+            xrecv.at[e, kind, chunk],
+            (there, core),
+        )
+
+    def held(e, kind, chunk):
+        return win.at[e, kind, piece(chunk)]
+
+    def hop_x(e, chunk):
+        return hop(e, FROM_X, chunk, own_rows(e, chunk), x_next)
+
+    def hop_y(e, chunk):
+        return hop(e, FROM_Y, chunk, own_rows(e, chunk), y_next)
+
+    def hop_z(e, chunk):
+        return hop(e, FROM_Z, chunk, held(e, FROM_Y, chunk), z_to)
+
+    def hop_relay(e, chunk):
+        return hop(e, RELAY, chunk, held(e, FROM_X, chunk), z_from)
+
+    def hop_last_early(e, chunk):
+        return hop(e, FROM_LAST, chunk, held(e, 1 - core, chunk), last_next)
+
+    def hop_last_late(e, chunk):
+        return hop(e, FROM_LAST, chunk, held(e, 2 + 2 * core, chunk), last_next)
+
+    def send_own(e):
+        for chunk in range(CHUNKS):
+            hop_y(e, chunk).start()
+            hop_x(e, chunk).start()
+
+    def first_hop(e, chunk):
+        hop_y(e, chunk).wait_recv()
+        pl.when(to_ok)(hop_z(e, chunk).start)
+        hop_x(e, chunk).wait_recv()
+        pl.when(level_chip)(hop_last_early(e, chunk).start)
+        pl.when(relay_send)(hop_relay(e, chunk).start)
+
+    def second_hop(e, chunk):
+        pl.when(from_ok)(hop_z(e, chunk).wait_recv)
+        pl.when(relay_recv)(hop_relay(e, chunk).wait_recv)
+        pl.when(later_ok)(hop_last_late(e, chunk).start)
+
+    def last_hop(e, chunk):
+        pl.when(last_ok)(hop_last_early(e, chunk).wait_recv)
+
+    def all_sent(e):
+        for chunk in range(CHUNKS):
+            hop_x(e, chunk).wait_send()
+            hop_y(e, chunk).wait_send()
+            pl.when(to_ok)(hop_z(e, chunk).wait_send)
+            pl.when(relay_send)(hop_relay(e, chunk).wait_send)
+            pl.when(level_chip)(hop_last_early(e, chunk).wait_send)
+            pl.when(later_ok)(hop_last_late(e, chunk).wait_send)
+
+    def pick(e, units, fresh=False):
+        which = e % 2
+        moves = {}
+        for index, (kind, chunk) in enumerate(units):
+            if kind == OWN and e >= 2:
+                continue
+            src = own_rows(e, chunk) if kind == OWN else held(e, kind, chunk)
+            moves[index] = pltpu.make_async_copy(src, stage.at[index], ssem.at[index])
+            when(arrived[kind], moves[index].start)
+        for index, (kind, chunk) in enumerate(units):
+
+            def add(index=index, kind=kind, chunk=chunk):
+                if index in moves:
+                    moves[index].wait()
+                offset = offsets[kind]
+
+                @pl.loop(0, rows // tile)
+                def _(step):
+                    r = at(step, tile)
+                    if e < 2:
+                        wanted = rel[r, :] - (offset * rows + chunk * part_rows)
+                        places = lax.broadcasted_iota(jnp.int32, (tile, part_rows), 1)
+                        hit = places == wanted
+                    else:
+                        wanted = sources[offset + 2, :, pl.ds(chunk * part_rows, part_rows)]
+                        places = lax.broadcasted_iota(jnp.int32, (tile, part_rows), 0)
+                        hit = places == wanted - (step * tile + seq * rows)
+                    chosen = jnp.where(hit, 1.0, 0.0).astype(BF16)
+                    block_rows = stage[index] if index in moves else block[e - 2, piece(chunk), :]
+                    value = inner(chosen, block_rows).astype(BF16)
+                    if fresh and index == 0:
+                        picked[which, r, :] = value
+                    else:
+                        picked[which, r, :] += value
+
+            when(arrived[kind], add)
+
+    def deliver(e):
+        target = (x, og)[e]
+        there = remote(picked.at[e, other_rows], target.at[:, mine], psend.at[e], precv.at[e], partner)
+        here = pltpu.make_async_copy(picked.at[e, keep], target.at[:, mine], plocal.at[e])
+        return there, here
+
+    def collect(e):
+        array = (og, in_low)[e - 2]
+        there = remote(array.at[:, theirs], block.at[e - 2, keep], psend.at[e], precv.at[e], partner)
+        here = pltpu.make_async_copy(array.at[:, mine], block.at[e - 2, keep], plocal.at[e])
+        return there, here
+
+    def bring_home(e):
+        target = (out_home, in_home)[e - 2]
+        there = remote(picked.at[e - 2], target.at[:, mine], hsend.at[e - 2], hrecv.at[e - 2], partner)
+        here = pltpu.make_async_copy(picked.at[e - 2], target.at[:, mine], hlocal.at[e - 2])
+        return there, here
+
+    def begin(pair):
+        for copy in pair:
+            copy.start()
+
+    def end(pair):
+        for copy in pair:
+            copy.wait()
+
+    orders = ((0, 1, 3, 2), (1, 0, 3, 2))
+    gots = (got0, got1, got2, got3)
+    span = mine_g.shape[-1]
+    part_span = span // PARTS
+
+    def part_cols(part):
+        return pl.ds(part * part_span, part_span)
+
+    def own_bit(bit):
+        return (seq // (1 << bit)) % 2
+
+    def halving(group, part, level):
+        order = orders[part]
+        index = []
+        for bit in (3, 2, 1, 0):
+            if bit in order[:level]:
+                index.append(own_bit(bit))
+            elif bit == order[level]:
+                index.append(1 - own_bit(bit))
+            else:
+                index.append(slice(None))
+        src = mine_g.at[(group, *index, slice(None), part_cols(part))]
+        dst = gots[level].at[group, part]
+        return remote(
+            src, dst, rsend.at[group, part, level], rrecv.at[group, part, level], across(order[level])
+        )
+
+    def halving_end(group, part, level):
+        halving(group, part, level).wait()
+        order = orders[part]
+        left = [bit for bit in (3, 2, 1, 0) if bit not in order[: level + 1]]
+        cols = part_cols(part)
+
+        @pl.loop(0, 1 << len(left))
+        def _(step):
+            digits = {bit: (step // (1 << (len(left) - 1 - i))) % 2 for i, bit in enumerate(left)}
+            place = [digits[bit] if bit in digits else own_bit(bit) for bit in (3, 2, 1, 0)]
+            value = mine_g[(group, *place, slice(None), cols)].astype(F32)
+            other = gots[level][(group, part, *[digits[bit] for bit in left])]
+            value = value + other.astype(F32)
+            if level == BITS - 1:
+                grad_sum[:, pl.ds(group * span + part * part_span, part_span)] = value
+            else:
+                mine_g[(group, *place, slice(None), cols)] = value.astype(BF16)
+
+    def advance(group, level):
+        for part in range(PARTS):
+            halving_end(group, part, level)
+            if level + 1 < BITS:
+                halving(group, part, level + 1).start()
+
+    def core_move(group, part):
+        cols = part_cols(part)
+        return remote(
+            give.at[:, :, :, :, :, cols],
+            from_core.at[group % 2, :, :, :, :, :, cols],
+            gsend.at[group, part],
+            grecv.at[group, part],
+            partner,
+        )
+
+    chunk_rows = give.shape[4]
+    m_rows = model // 2
+
+    def group_products(group, columns):
+        if group == 2:
+            pl.semaphore_wait(credit, 1)
+        for side in (0, 1):
+            for part in range(PARTS):
+                if side == 0 and group > 0:
+                    core_move(group - 1, part).wait_send()
+                if side == 1:
+                    core_move(group, part).wait_recv()
+                place = 0
+                for left, right, start, size in columns(part, (1 - core, core)[side]):
+                    cols = pl.ds(part * part_span + place, size)
+                    place += size
+
+                    @pl.loop(0, 2)
+                    def _(m, left=left, right=right, start=start, size=size, cols=cols):
+                        value = inner(left[at(m, m_rows), :], right[:, pl.ds(start, size)])
+                        value = value.reshape(2, 2, 2, chunk_rows, size)
+                        if side == 0:
+                            give[m, :, :, :, :, cols] = value.astype(BF16)
+                        else:
+                            value = value + from_core[group % 2, m, :, :, :, :, cols].astype(F32)
+                            mine_g[group, m, :, :, :, :, cols] = value.astype(BF16)
+
+                if side == 0:
+                    core_move(group, part).start()
+                else:
+                    halving(group, part, 0).start()
+        if group == 0:
+            pl.semaphore_signal(credit, inc=1, device_id=partner, device_id_type=MESH)
+
+    part_out = 2 * model + hidden
+
+    def sum_move(level):
+        device = partner if level == 0 else across(level - 1)
+        return remote(vsend.at[level], vrecv.at[level], vsem.at[0, level], vsem.at[1, level], device)
+
+    def sum_next(level):
+        sum_move(level).wait()
+        value = vsend[level] + vrecv[level]
+        if level == BITS:
+            sums_sum[...] = value
+        else:
+            vsend[level + 1] = value
+            sum_move(level + 1).start()
+
+    send_own(0)
+    sources[2] = source[...]
+    tinies = []
+    for offset in OFFSETS[1:]:
+        device, there_ok = others[offset]
+        out = remote(source, sources.at[2 - offset], ssend.at[2 - offset], srecv.at[2 - offset], device)
+        back = remote(source, sources.at[2 + offset], ssend.at[2 + offset], srecv.at[2 + offset], device)
+        pl.when(there_ok)(out.start)
+        tinies.append((there_ok, out, back))
+
+    wide, deep = wq.shape[1], wd_half.shape[0]
+    pieces = []
+    for i, array in enumerate((wq, wk, wv)):
+        pieces.append((array, wqkv.at[:, pl.ds(pl.multiple_of(i * model + core * wide, wide), wide)]))
+    pieces.append((wo_half, wo.at[at(core, wide), :]))
+    pieces.append((wu_half, wu.at[:, at(core, deep)]))
+    pieces.append((wd_half, wd.at[at(core, deep), :]))
+    pieces.append((bq, bqkv.at[:, at(core, wide)]))
+    pieces.append((bv, bqkv.at[:, pl.ds(pl.multiple_of(2 * model + core * wide, wide), wide)]))
+    pieces.append((bu_half, bu.at[:, at(core, deep)]))
+    weights = []
+    for i, (array, place) in enumerate(pieces):
+        there = remote(array, place, wsend.at[i], wrecv.at[i], partner)
+        here = pltpu.make_async_copy(array, place, wlocal.at[i])
+        begin((there, here))
+        weights.append((there, here))
+    bqkv[:, pl.ds(model, model)] = jnp.zeros((1, model), F32)
+
+    pick(0, [(OWN, 0), (OWN, 1)], fresh=True)
+    pick(1, [(OWN, 0), (OWN, 1)], fresh=True)
+    first_hop(0, 0)
+    pick(0, [(FROM_X, 0), (FROM_Y, 0)])
+    first_hop(0, 1)
+    second_hop(0, 0)
+    pick(0, [(FROM_X, 1), (FROM_Y, 1), (FROM_Z, 0)])
+    second_hop(0, 1)
+    send_own(1)
+    last_hop(0, 0)
+    pick(0, [(FROM_Z, 1), (FROM_LAST, 0)])
+    last_hop(0, 1)
+    pick(0, [(FROM_LAST, 1)])
+    begin(deliver(0))
+    for pair in weights:
+        end(pair)
+    end(deliver(0))
+
+    lanes = lax.broadcasted_iota(jnp.int32, (CLUSTER, 128), 1)
+    first_f = jnp.where(lanes < HEAD_DIM, 1.0, 0.0)
+    first = first_f.astype(BF16)
+    second = (1.0 - first_f).astype(BF16)
+
+    def stacked(pair):
+        return jnp.concatenate([pair * first, pair * second], axis=0)
+
+    def beside(tall):
+        return jnp.concatenate([tall[:CLUSTER], tall[CLUSTER:]], axis=1)
+
+    @pl.loop(0, 3 * model // tile)
+    def _(step):
+        cols = at(step, tile)
+        qkv[:, cols] = (inner(x[...], wqkv[:, cols]) + bqkv[:, cols]).astype(BF16)
+
+    first_hop(1, 0)
+
+    @pl.loop(0, clusters)
+    def _(cluster):
+        r = at(cluster, CLUSTER)
+        for pair in range(pairs):
+            q = qkv[r, pl.ds(pair * 128, 128)]
+            k = qkv[r, pl.ds(model + pair * 128, 128)]
+            v = qkv[r, pl.ds(2 * model + pair * 128, 128)]
+            scores = outer(stacked(q), k) * score_scale
+            scores = jnp.where(valid[cluster] > 0.5, scores, masked_score)
+            top = jnp.max(scores, axis=-1, keepdims=True)
+            weight = jnp.exp(scores - top)
+            p = weight * (1.0 / jnp.sum(weight, axis=-1, keepdims=True))
+            prob[cluster * pairs + pair] = p
+            ctx[r, pl.ds(pair * 128, 128)] = inner(beside(p.astype(BF16)), stacked(v)).astype(BF16)
+
+    first_hop(1, 1)
+
+    @pl.loop(0, model // tile)
+    def _(step):
+        cols = at(step, tile)
+        hat1[:, cols] = inner(ctx[...], wo[:, cols]) + x[:, cols].astype(F32) + bo[:, cols]
+
+    @pl.loop(0, half // band)
+    def _(step):
+        r = at(step, band)
+        h = hat1[r, :]
+        centered = h - jnp.mean(h, axis=-1, keepdims=True)
+        inv = lax.rsqrt(jnp.mean(centered * centered, axis=-1, keepdims=True) + norm_eps)
+        hat = centered * inv
+        hat1[r, :] = hat
+        inv1[r, :] = inv
+        low1[r, :] = (hat * g1[...] + s1[...]).astype(BF16)
+
+    second_hop(1, 0)
+
+    @pl.loop(0, hidden // tile)
+    def _(step):
+        cols = at(step, tile)
+        pre = inner(low1[...], wu[:, cols]) + bu[:, cols]
+        cdf = 0.5 * (1.0 + lax.erf(pre * root_half))
+        act[:, cols] = (pre * cdf).astype(BF16)
+        slope[:, cols] = cdf + pre * jnp.exp(-0.5 * pre * pre) * inv_root_tau
+
+    second_hop(1, 1)
+
+    @pl.loop(0, model // tile)
+    def _(step):
+        cols = at(step, tile)
+        norm = hat1[:, cols] * g1[:, cols] + s1[:, cols]
+        work[:, cols] = inner(act[...], wd[:, cols]) + norm + bd[:, cols]
+
+    pick(1, [(FROM_X, 0), (FROM_Y, 0), (FROM_X, 1), (FROM_Y, 1)])
+    last_hop(1, 0)
+    last_hop(1, 1)
+    pick(1, [(FROM_Z, 0), (FROM_Z, 1), (FROM_LAST, 0), (FROM_LAST, 1)])
+    begin(deliver(1))
+    end(deliver(1))
+
+    accs[...] = jnp.zeros_like(accs)
+
+    @pl.loop(0, half // band)
+    def _(step):
+        r = at(step, band)
+        h = work[r, :]
+        centered = h - jnp.mean(h, axis=-1, keepdims=True)
+        inv = lax.rsqrt(jnp.mean(centered * centered, axis=-1, keepdims=True) + norm_eps)
+        hat = centered * inv
+        grad = og[r, :].astype(F32)
+        og[r, :] = (hat * g2[...] + s2[...]).astype(BF16)
+        accs[4] += fold_rows(grad * hat)
+        accs[5] += fold_rows(grad)
+        scaled = grad * g2[...]
+        back = inv * (
+            scaled
+            - jnp.mean(scaled, axis=-1, keepdims=True)
+            - hat * jnp.mean(scaled * hat, axis=-1, keepdims=True)
+        )
+        accs[3] += fold_rows(back)
+        work[r, :] = back
+        low2[r, :] = back.astype(BF16)
+
+    begin(collect(2))
+
+    def flip(source_rows, target=flipped):
+        @pl.loop(0, model // 128)
+        def _(step):
+            target[at(step, 128), :] = source_rows[:, at(step, 128)].T
+
+    def long_columns(part, side):
+        start = pl.multiple_of(side * span + part * part_span, part_span)
+        return [(flipped, act, start, part_span)]
+
+    flip(low2)
+    end(collect(2))
+    send_own(2)
+    group_products(0, long_columns)
+
+    @pl.loop(0, hidden // tile)
+    def _(step):
+        cols = at(step, tile)
+        back = outer(low2[...], wd[cols, :]) * slope[:, cols]
+        back = back.astype(BF16)
+        act[:, cols] = back
+        vsend[0, :, pl.ds(pl.multiple_of(2 * model + step * tile, tile), tile)] = jnp.sum(
+            back.astype(F32), axis=0, keepdims=True
+        )
+
+    first_hop(2, 0)
+    flip(low1)
+    group_products(1, long_columns)
+    first_hop(2, 1)
+
+    @pl.loop(0, model // tile)
+    def _(step):
+        cols = at(step, tile)
+        work[:, cols] += outer(act[...], wu[cols, :])
+
+    @pl.loop(0, half // band)
+    def _(step):
+        r = at(step, band)
+        grad = work[r, :]
+        hat = hat1[r, :]
+        accs[1] += fold_rows(grad * hat)
+        accs[2] += fold_rows(grad)
+        scaled = grad * g1[...]
+        back = inv1[r, :] * (
+            scaled
+            - jnp.mean(scaled, axis=-1, keepdims=True)
+            - hat * jnp.mean(scaled * hat, axis=-1, keepdims=True)
+        )
+        accs[0] += fold_rows(back)
+        work[r, :] = back
+        low2[r, :] = back.astype(BF16)
+
+    second_hop(2, 0)
+
+    @pl.loop(0, model // tile)
+    def _(step):
+        cols = at(step, tile)
+        low1[:, cols] = outer(low2[...], wo[cols, :]).astype(BF16)
+
+    advance(0, 0)
+    second_hop(2, 1)
+
+    @pl.loop(0, clusters)
+    def _(cluster):
+        r = at(cluster, CLUSTER)
+        for pair in range(pairs):
+            at_q = pl.ds(pair * 128, 128)
+            at_k = pl.ds(model + pair * 128, 128)
+            at_v = pl.ds(2 * model + pair * 128, 128)
+            q, k, v = qkv[r, at_q], qkv[r, at_k], qkv[r, at_v]
+            p = prob[cluster * pairs + pair]
+            dctx = stacked(low1[r, at_q])
+            dprob = outer(dctx, v)
+            dscore = (p * (dprob - jnp.sum(p * dprob, axis=-1, keepdims=True))).astype(BF16)
+            act[r, at_q] = (inner(beside(dscore), stacked(k)) * score_scale).astype(BF16)
+            act[r, at_k] = (under(dscore, stacked(q)) * score_scale).astype(BF16)
+            act[r, at_v] = under(p.astype(BF16), dctx).astype(BF16)
+
+    dqkv = act.at[:, pl.ds(0, 3 * model)]
+
+    @pl.loop(0, model // tile)
+    def _(step):
+        cols = at(step, tile)
+        in_low[:, cols] = (work[:, cols] + outer(dqkv[...], wqkv[cols, :])).astype(BF16)
+
+    begin(collect(3))
+    advance(0, 1)
+    advance(1, 0)
+    end(collect(3))
+    send_own(3)
+
+    for which in range(2):
+        @pl.loop(0, model // tile)
+        def _(step, which=which):
+            value = act[:, pl.ds(pl.multiple_of(2 * which * model + step * tile, tile), tile)]
+            vsend[0, :, pl.ds(pl.multiple_of(which * model + step * tile, tile), tile)] = jnp.sum(
+                value.astype(F32), axis=0, keepdims=True
+            )
+
+    for i in range(6):
+        vsend[0, :, pl.ds(part_out + i * model, model)] = jnp.sum(accs[i], axis=0, keepdims=True)
+    sum_move(0).start()
+
+    flip(low2)
+    flip(x, flipped_x)
+
+    def square_columns(part, side):
+        start = pl.multiple_of(side * width, width)
+        if part == 0:
+            return [(flipped, ctx, start, width), (flipped_x, act, start, width)]
+        return [
+            (flipped_x, act, pl.multiple_of(model + side * width, width), width),
+            (flipped_x, act, pl.multiple_of(2 * model + side * width, width), width),
+        ]
+
+    group_products(2, square_columns)
+    first_hop(3, 0)
+    advance(0, 2)
+    advance(1, 1)
+    first_hop(3, 1)
+    second_hop(3, 0)
+    sum_next(0)
+    for there_ok, out, back in tinies:
+
+        def finish(out=out, back=back):
+            out.wait_send()
+            back.wait_recv()
+
+        pl.when(there_ok)(finish)
+    last_hop(2, 0)
+    last_hop(2, 1)
+    pick(2, [(OWN, 0), (OWN, 1)], fresh=True)
+    pick(2, [(FROM_X, 0), (FROM_Y, 0), (FROM_X, 1), (FROM_Y, 1)])
+    second_hop(3, 1)
+    sum_next(1)
+    advance(2, 0)
+    pick(2, [(FROM_Z, 0), (FROM_Z, 1), (FROM_LAST, 0), (FROM_LAST, 1)])
+    begin(bring_home(2))
+    advance(0, 3)
+    advance(1, 2)
+    sum_next(2)
+    pick(3, [(OWN, 0), (OWN, 1)], fresh=True)
+    pick(3, [(FROM_X, 0), (FROM_Y, 0), (FROM_X, 1), (FROM_Y, 1)])
+    advance(2, 1)
+    advance(1, 3)
+    sum_next(3)
+    last_hop(3, 0)
+    pick(3, [(FROM_Z, 0), (FROM_Z, 1), (FROM_LAST, 0)])
+    last_hop(3, 1)
+    pick(3, [(FROM_LAST, 1)])
+    begin(bring_home(3))
+    advance(2, 2)
+    sum_next(4)
+    advance(2, 3)
+    for part in range(PARTS):
+        core_move(2, part).wait_send()
+    for e in range(EXCHANGES):
+        all_sent(e)
+    end(bring_home(2))
+    end(bring_home(3))
+
+
+def whole(mesh, *args):
+    tokens, wu_half = args[0], args[9]
+    rows, model = tokens.shape
+    half, width = rows // 2, model // 2
+    hidden = 2 * wu_half.shape[1]
+    blocks = mesh.shape["seq"]
+    hbm = pl.BlockSpec(memory_space=pl.ANY)
+    vmem = pl.BlockSpec(memory_space=pltpu.VMEM)
+    dma = pltpu.SemaphoreType.DMA
+    chunk = model // blocks
+    span = 4 * width
+    part_span = span // PARTS
+    steps = half // CLUSTER * (model // 128)
+    total = 8 * model + hidden
+    cube = (2, 2, 2, 2)
+    return pl.pallas_call(
+        functools.partial(whole_kernel, blocks),
+        out_shape=(
+            jax.ShapeDtypeStruct((rows, model), BF16),
+            jax.ShapeDtypeStruct((rows, model), BF16),
+            jax.ShapeDtypeStruct((chunk, GROUPS * span), F32),
+            jax.ShapeDtypeStruct((1, total), F32),
+            jax.ShapeDtypeStruct((EXCHANGES, 5, rows, width), BF16),
+        ),
+        in_specs=[hbm, hbm, vmem, vmem, vmem] + [hbm] * 9 + [vmem] * 6,
+        out_specs=(hbm, hbm, vmem, vmem, hbm),
+        scratch_shapes=[
+            pltpu.VMEM((model, 3 * model), BF16),
+            pltpu.VMEM((model, model), BF16),
+            pltpu.VMEM((model, hidden), BF16),
+            pltpu.VMEM((hidden, model), BF16),
+            pltpu.VMEM((1, 3 * model), F32),
+            pltpu.VMEM((1, hidden), F32),
+            pltpu.VMEM((4, rows // CHUNKS, width), BF16),
+            pltpu.VMEM((2, rows, width), BF16),
+            pltpu.VMEM((2, rows, width), BF16),
+            pltpu.VMEM((5, 1, rows), jnp.int32),
+            pltpu.VMEM((half, model), BF16),
+            pltpu.VMEM((half, model), BF16),
+            pltpu.VMEM((half, 3 * model), BF16),
+            pltpu.VMEM((half, model), BF16),
+            pltpu.VMEM((steps, 2 * CLUSTER, CLUSTER), F32),
+            pltpu.VMEM((half, model), F32),
+            pltpu.VMEM((half, 1), F32),
+            pltpu.VMEM((half, model), BF16),
+            pltpu.VMEM((half, hidden), BF16),
+            pltpu.VMEM((half, hidden), F32),
+            pltpu.VMEM((half, model), F32),
+            pltpu.VMEM((model, half), BF16),
+            pltpu.VMEM((model, half), BF16),
+            pltpu.VMEM((half, model), BF16),
+            pltpu.VMEM((half, model), BF16),
+            pltpu.VMEM((6, 8, model), F32),
+            pltpu.VMEM((GROUPS,) + cube + (chunk, span), BF16),
+            pltpu.VMEM((2,) + cube + (chunk, span), BF16),
+            pltpu.VMEM(cube + (chunk, span), BF16),
+            pltpu.VMEM((GROUPS, PARTS, 2, 2, 2, chunk, part_span), BF16),
+            pltpu.VMEM((GROUPS, PARTS, 2, 2, chunk, part_span), BF16),
+            pltpu.VMEM((GROUPS, PARTS, 2, chunk, part_span), BF16),
+            pltpu.VMEM((GROUPS, PARTS, chunk, part_span), BF16),
+            pltpu.VMEM((BITS + 1, 1, total), F32),
+            pltpu.VMEM((BITS + 1, 1, total), F32),
+            dma((9,)),
+            dma((9,)),
+            dma((9,)),
+            dma((EXCHANGES, 5, CHUNKS)),
+            dma((EXCHANGES, 5, CHUNKS)),
+            dma((5,)),
+            dma((5,)),
+            dma((4,)),
+            dma((EXCHANGES,)),
+            dma((EXCHANGES,)),
+            dma((EXCHANGES,)),
+            dma((2,)),
+            dma((2,)),
+            dma((2,)),
+            dma((GROUPS, PARTS)),
+            dma((GROUPS, PARTS)),
+            dma((GROUPS, PARTS, BITS)),
+            dma((GROUPS, PARTS, BITS)),
+            dma((2, BITS + 1)),
+            pltpu.SemaphoreType.REGULAR,
+        ],
+        compiler_params=pltpu.CompilerParams(
+            collective_id=2, has_side_effects=True, vmem_limit_bytes=64 * MEBI
+        ),
+    )(*args)[:4]
+
+
 def body(
     mesh,
     tokens,
@@ -912,55 +1700,86 @@
     def row(v):
         return v.reshape(1, -1)
 
-    x, og, sources, wqkv, wo, wu, wd, bqkv, bu = entry(
-        mesh,
-        tokens,
-        out_grad,
-        (source - seq * rows).reshape(rows, 1),
-        row(source),
-        query_weight,
-        key_weight,
-        value_weight,
-        output_weight,
-        up_weight,
-        down_weight,
-        row(query_bias),
-        row(value_bias),
-        row(up_bias),
-    )
-    no_key = (jnp.arange(3 * model) // model != 1)[None, :]
-    bqkv = jnp.where(no_key, bqkv, 0.0)
+    rel = (source - seq * rows).reshape(rows, 1)
     chunk = model // blocks
-    reduce = chunk % 16 == 0 and blocks >= 4 and blocks & (blocks - 1) == 0
-    out_low, in_low, grads, sums = layer(
-        chunk if reduce else 48,
-        x,
-        og,
-        valid,
-        wqkv,
-        wo,
-        wu,
-        wd,
-        bqkv,
-        row(output_bias),
-        row(first_gain),
-        row(first_shift),
-        bu,
-        row(down_bias),
-        row(second_gain),
-        row(second_shift),
-    )
-    if reduce:
-        out_home, in_home, grad_sum, sums = leave(mesh, True, out_low, in_low, sources, grads, sums)
+    part_q, part_h = model // 2, hidden // 2
+    order = ("q", "k", "v", "o", "up", "down")
+    if blocks == 1 << BITS and chunk % 16 == 0 and hidden == 4 * model:
+        order = ("down", "up", "o", "q", "k", "v")
+        out_home, in_home, grad_sum, sums = whole(
+            mesh,
+            tokens,
+            out_grad,
+            rel,
+            row(source),
+            valid,
+            query_weight,
+            key_weight,
+            value_weight,
+            output_weight,
+            up_weight,
+            down_weight,
+            row(query_bias),
+            row(value_bias),
+            row(up_bias),
+            row(output_bias),
+            row(first_gain),
+            row(first_shift),
+            row(down_bias),
+            row(second_gain),
+            row(second_shift),
+        )
     else:
-        out_home, in_home = leave(mesh, False, out_low, in_low, sources, None, None)
-        sums = lax.psum(sums, ("seq", "head"))
-        grads = grads.reshape(2, model, -1)
-        grads = lax.psum_scatter(grads.astype(F32), "head", scatter_dimension=0, tiled=True)[0]
-        grad_sum = lax.psum_scatter(grads, "seq", scatter_dimension=0, tiled=True)
-    part_q, part_h = model // 2, hidden // 2
-    cuts = [part_q * i for i in range(5)] + [4 * part_q + part_h, 4 * part_q + 2 * part_h]
-    dwq, dwk, dwv, dwo, dwu, dwd = (grad_sum[:, a:b] for a, b in zip(cuts[:-1], cuts[1:]))
+        x, og, sources, wqkv, wo, wu, wd, bqkv, bu = entry(
+            mesh,
+            tokens,
+            out_grad,
+            rel,
+            row(source),
+            query_weight,
+            key_weight,
+            value_weight,
+            output_weight,
+            up_weight,
+            down_weight,
+            row(query_bias),
+            row(value_bias),
+            row(up_bias),
+        )
+        no_key = (jnp.arange(3 * model) // model != 1)[None, :]
+        bqkv = jnp.where(no_key, bqkv, 0.0)
+        reduce = chunk % 16 == 0 and blocks >= 4 and blocks & (blocks - 1) == 0
+        out_low, in_low, grads, sums = layer(
+            chunk if reduce else 48,
+            x,
+            og,
+            valid,
+            wqkv,
+            wo,
+            wu,
+            wd,
+            bqkv,
+            row(output_bias),
+            row(first_gain),
+            row(first_shift),
+            bu,
+            row(down_bias),
+            row(second_gain),
+            row(second_shift),
+        )
+        if reduce:
+            out_home, in_home, grad_sum, sums = leave(mesh, True, out_low, in_low, sources, grads, sums)
+        else:
+            out_home, in_home = leave(mesh, False, out_low, in_low, sources, None, None)
+            sums = lax.psum(sums, ("seq", "head"))
+            grads = grads.reshape(2, model, -1)
+            grads = lax.psum_scatter(grads.astype(F32), "head", scatter_dimension=0, tiled=True)[0]
+            grad_sum = lax.psum_scatter(grads, "seq", scatter_dimension=0, tiled=True)
+    grad_of, place = {}, 0
+    for name in order:
+        size = part_h if name in ("up", "down") else part_q
+        grad_of[name] = grad_sum[:, place : place + size]
+        place += size
     sums = sums[0]
 
     def mine(start, size):
@@ -972,18 +1791,18 @@
     return (
         out_home.astype(F32),
         in_home.astype(F32),
-        dwq,
+        grad_of["q"],
         mine(0, part_q),
-        dwk,
-        dwv,
+        grad_of["k"],
+        grad_of["v"],
         mine(model, part_q),
-        dwo.T,
+        grad_of["o"].T,
         block(0),
         block(1),
         block(2),
-        dwu,
+        grad_of["up"],
         mine(2 * model, part_h),
-        dwd.T,
+        grad_of["down"].T,
         block(3),
         block(4),
         block(5),

time: 454 us -> 263 us (0.58)
  Pallas kernels: 418 us -> 232 us
  local copies, waits for them, and re-layouts: 26.3 us -> 20.6 us
    pallas_call x3 -> x1, Pallas kernels: 418 us -> 232 us  [whole(): pl.pallas_call(functools.partial(whole_kernel, blocks), out_shape=(jax.Sh...]
    unnamed x44 -> x4, local copies, waits for them, and re-layouts: 14.4 us -> 0.06 us
    reshape x9, local copies, waits for them, and re-layouts: 5.59 us -> 11.4 us  [row(): return v.reshape(1, -1)]
where the time goes in v2:
time: 263 us; the launch traced here: 262 us
  Pallas kernels  232 us (88%)
  local copies, waits for them, and re-layouts  20.6 us (8%)
  other arithmetic  8.14 us (3%)
    pallas_call x1, Pallas kernels, whole(): pl.pallas_call(functools.partial(whole_kernel, blocks), out_shape=(jax.Sh...  232 us
    reshape x9, local copies, waits for them, and re-layouts, row(): return v.reshape(1, -1)  11.4 us

profile of v2, /device:TPU:0, one launch (start us, length us, event | category | flops | bytes accessed | tf_op | source)
XLA Modules:
  0.0 261.7 jit_solution(16880304112461733622)
XLA Ops:
  0.7 0.7 fusion.9
  1.3 0.2 reduce-window.9
  1.5 0.7 bitcast_subtract_fusion
  2.2 0.1 convert_reduce_fusion
  2.3 0.8 select_reduce_fusion
  3.1 0.7 compare_convert_fusion
  3.7 0.6 constant_dynamic-slice_fusion.7
  4.3 1.3 broadcast_subtract_fusion
  5.6 1.0 copy.37.rel
  6.6 1.3 reshape.125.bu_half
  7.9 1.3 reshape.126.bo
  9.2 1.3 reshape.127.g1
  10.5 1.3 reshape.128.s1
  11.7 1.3 reshape.129.bd
  13.0 1.3 reshape.130.g2
  14.3 1.3 reshape.131.s2
  15.5 1.2 reshape.123.bq
  16.8 1.2 reshape.124.bv
  18.0 232.2 %shard_map.314 = (bf16[1024,768]{1,0:T(8,128)(2,1)}, bf16[1024,768]{1,0:T(8,128)(2,1)}, f32[48,4608]{1,0:T(8,128)}, f32[1,9216]{1,0:T(1,128)}, bf16[4,5,1024,384]{3,2,1,0:T(8,128)(2,1)}) custom-call(bf16[1024,768]{1,0:T(8,128)(2,1)} %tokens.1, bf16[1024,768]{1,0:T(8,128)(2,1)} %out_grad.1, s32[1024,1]{1,0:T(8,128)} %copy.37.rel, s32[1,1024]{1,0:T(1,128)} %bitcast.24, ...), custom_call_target="tpu_custom_call" | custom-call | tf_op jit(solution)/shard_map/pallas_call | solution.py:1593
  250.2 0.0 copy-start.1
  250.2 1.4 fusion.2
  251.7 1.3 fusion.1
  253.0 1.3 dynamic-slice_reduce_fusion
  254.3 1.7 slice_bitcast_fusion.1
  256.0 1.9 slice_bitcast_fusion
  257.9 0.0 copy-done.1
  257.9 0.0 copy-start
  257.9 1.9 convert_element_type.11
  259.8 0.1 copy-done
  259.8 1.9 convert_element_type.12
  (2 shorter events, 0.0 us)
Async XLA Ops:
  250.2 7.6 %copy-start.1 = (bf16[1024,768]{1,0:T(8,128)(2,1)S(1)}, bf16[1024,768]{1,0:T(8,128)(2,1)}, u32[]{:S(2)}) copy-start(bf16[1024,768]{1,0:T(8,128)(2,1)} %get-tuple-element.21) | copy-start | bytes 4718596
  257.9 2.0 copy-start
